TPU v7x, 128 devices: a whole 4x4x4 slice. The times are simulated.
128 devices in a mesh: rotor: 8 (over y, core), tower: 16 (over z, x).
Axes of the slice: x: 4, y: 4, z: 4, core: 2. Of those that a mesh axis runs over, the one named last changes fastest.
Arguments:
- solution: float32 [2, 5, 2, 16, 64, 4096], P(None, None, None, 'rotor', None, 'tower'), may hold values from -0.5 to 2.8, as said below
- fringe_owner: int32 [8, 16, 2, 128, 1], P('rotor', 'tower'), may hold values from 0 to 127; in each aligned block of 128 rows (0 to 127, 128 to 255, ..., all dimensions but the last counted through in order) at most 2 rows name the same one
- fringe_donor: int32 [8, 16, 2, 128], P('rotor', 'tower'), may hold values from 0 to 1023, as said below
- fringe_target: int32 [8, 16, 2, 128], P('rotor', 'tower'), may hold values from 0 to 65535, as said below
- fringe_weight: float32 [8, 16, 2, 128, 64], P('rotor', 'tower'), may hold values from 0.01171875 to 0.01953125
Outputs:
- advanced: float32 [2, 5, 2, 16, 64, 4096], P(None, None, None, 'rotor', None, 'tower')
Inputs may be any that keep to these rules, and one draw needn't show every extreme that they name: `fringe_owner`: in the fringe list of one device for one section at most 2 points have the same owner, and some owner has exactly 2. `fringe_donor`: the donor's grid differs from the grid of the point's target. `fringe_target`: the targets of one device's list for one section are distinct. `solution`: in field 0 density and pressure lie in 0.9 to 1.1 and each velocity component in -0.15 to 0.15; field 1 lies in -0.5 to 0.6.
All inputs are finite; a program needn't handle non-finite values.
Results may differ from a plain program's by a relative error of at most 0.0003.
Values sent between devices are 32-bit elements; how exact they have to be, the bound alone decides.
No kernel may reach another device: no remote copies, remote signals or barrier semaphores. Data moves between devices by JAX's collectives and lax.ppermute only.
A program may use at most 256 MiB of HBM per device.

v0:
```python
from functools import partial

import jax
import jax.numpy as jnp
import numpy as np
from jax import lax
from jax.experimental import pallas as pl
from jax.experimental.pallas import tpu as pltpu
from jax.sharding import PartitionSpec as P

DT = 0.01
DEV = 128
AXES = ("rotor", "tower")
F32, BF16, I32 = jnp.float32, jnp.bfloat16, jnp.int32
HIGH = lax.Precision.HIGHEST


def lagrange_values(nodes, at):
    values = np.ones(4)
    for j in range(4):
        for m in range(4):
            if m != j:
                values[j] *= (at - nodes[m]) / (nodes[j] - nodes[m])
    return values


def lagrange_slopes(nodes, at):
    slopes = np.zeros(4)
    for j in range(4):
        for k in range(4):
            if k != j:
                factor = 1.0 / (nodes[j] - nodes[k])
                for m in range(4):
                    if m != j and m != k:
                        factor *= (at - nodes[m]) / (nodes[j] - nodes[m])
                slopes[j] += factor
    return slopes


def expand(block, axis):
    pieces = [np.eye(4)] * 3
    pieces[axis] = block
    return np.kron(np.kron(pieces[0], pieces[1]), pieces[2])


NODES = np.array([-0.8611363115940526, -0.3399810435848563, 0.3399810435848563, 0.8611363115940526])
QUAD = np.array([0.3478548451374538, 0.6521451548625461, 0.6521451548625461, 0.3478548451374538])
SLOPES = np.stack([lagrange_slopes(NODES, at) for at in NODES])
LOW, HIGHV = lagrange_values(NODES, -1.0), lagrange_values(NODES, 1.0)
LIFT_LO, LIFT_HI = LOW / QUAD, HIGHV / QUAD


def halves(table):
    hi = table.astype(np.float32).astype(jnp.bfloat16)
    lo = (table - hi.astype(np.float64)).astype(jnp.bfloat16)
    return hi, lo


def tables():
    e_lo = [expand(LOW[None, :], d) for d in range(3)]
    e_hi = [expand(HIGHV[None, :], d) for d in range(3)]
    l_lo = [expand(LIFT_LO[:, None], d) for d in range(3)]
    l_hi = [expand(LIFT_HI[:, None], d) for d in range(3)]
    weak = [expand(SLOPES, d) - l_hi[d] @ e_hi[d] + l_lo[d] @ e_lo[d] for d in range(3)]
    main = np.concatenate(weak + [-l_lo[1], l_hi[1], -l_lo[2], l_hi[2]], axis=1)
    trace = np.concatenate([t for d in range(3) for t in (e_lo[d], e_hi[d])], axis=0)
    t_hi, t_lo = halves(trace)
    return main, np.concatenate([t_hi, t_hi, t_lo], axis=1)


MAIN, TRACE = tables()


def iota(shape, dim):
    return lax.broadcasted_iota(I32, shape, dim)


def dot(a, b, precision=None):
    return lax.dot_general(a, b, (((1,), (0,)), ((), ())), precision=precision, preferred_element_type=F32)


def split(x):
    hi = x.astype(BF16)
    return hi, (x - hi.astype(F32)).astype(BF16)


def pick4(index, values):
    out = jnp.full(index.shape, float(values[3]), F32)
    for i in range(3):
        out = jnp.where(index == i, float(values[i]), out)
    return out


def primitive(u):
    rho, m1, m2, m3, en = u
    r = 1.0 / rho
    v = [m1 * r, m2 * r, m3 * r]
    vv = v[0] * v[0] + v[1] * v[1] + v[2] * v[2]
    p = 0.4 * (en - 0.5 * rho * vv)
    return r, v, vv, p


def tangent(du, r, v, vv):
    dv = [(du[1 + i] - v[i] * du[0]) * r for i in range(3)]
    dp = 0.4 * (du[4] - (v[0] * du[1] + v[1] * du[2] + v[2] * du[3]) + 0.5 * vv * du[0])
    return dv, dp


def flux(u, du, v, p, dv, dp, d):
    out = [u[1 + d]]
    dout = [du[1 + d]]
    for i in range(3):
        f = u[1 + i] * v[d]
        df = du[1 + i] * v[d] + u[1 + i] * dv[d]
        if i == d:
            f, df = f + (p - 1.0), df + dp
        out.append(f)
        dout.append(df)
    out.append((u[4] + p) * v[d])
    dout.append((du[4] + dp) * v[d] + (u[4] + p) * dv[d])
    return out, dout


def side(w, d):
    u, du = w[:5], w[5:]
    r, v, vv, p = primitive(u)
    dv, dp = tangent(du, r, v, vv)
    f, df = flux(u, du, v, p, dv, dp, d)
    c2 = 1.4 * p * r
    dc2 = 1.4 * r * dp - c2 * r * du[0]
    s2 = v[d] * v[d] + c2
    r1, r2 = lax.rsqrt(c2), lax.rsqrt(s2)
    s = c2 * r1 + s2 * r2
    ds = 0.5 * dc2 * r1 + (v[d] * dv[d] + 0.5 * dc2) * r2
    return f + df, s, ds


def common(left, right, d):
    fl, sl, dsl = side(left, d)
    fr, sr, dsr = side(right, d)
    s, ds = 0.25 * (sl + sr), 0.25 * (dsl + dsr)
    out = []
    for i in range(5):
        out.append(0.5 * (fl[i] + fr[i]) - s * (right[i] - left[i]))
    for i in range(5):
        out.append(
            0.5 * (fl[5 + i] + fr[5 + i]) - ds * (right[i] - left[i]) - s * (right[5 + i] - left[5 + i])
        )
    return out, fl, fr


def request_kernel(owner, donor, target, weight, req, trow, tcol):
    sub, lane = iota((DEV, DEV), 0), iota((DEV, DEV), 1)
    results = []
    tc = [jnp.zeros((DEV, DEV), F32) for _ in range(2)]
    for sec in range(2):
        oc = jnp.broadcast_to(owner[0, 0, sec].astype(F32), (DEV, DEV))
        orow = oc.T
        same = (oc == orow) & (sub < lane)
        pos = jnp.sum(jnp.where(same, 1.0, 0.0), axis=0, keepdims=True)
        dc = jnp.broadcast_to(donor[0, 0, sec : sec + 1].astype(F32), (DEV, DEV)).T
        tg = jnp.broadcast_to(target[0, 0, sec : sec + 1].astype(F32) + 1.0, (DEV, DEV)).T
        w = jnp.concatenate([weight[0, 0, sec], jnp.zeros((DEV, 64), F32)], axis=1)
        rhs = jnp.where(lane == 64, dc, jnp.where(lane == 65, tg, w))
        for s in range(2):
            chosen = (orow == sub.astype(F32)) & (pos == float(s))
            res = dot(jnp.where(chosen, 1.0, 0.0), rhs, HIGH)
            results.append(res)
            tc[s] = jnp.where(lane == sec, res[:, 65:66], tc[s])
    for sec in range(2):
        pair = jnp.where(lane < 64, results[2 * sec], pltpu.roll(results[2 * sec + 1], 64, 1))
        req[:, sec * 128 : sec * 128 + 128] = pair
    ids = jnp.zeros((DEV, DEV), F32)
    for i in range(4):
        ids = jnp.where(lane == i, results[i][:, 64:65], ids)
    req[:, 256:384] = ids
    for s in range(2):
        tcol[s * 128 : s * 128 + 128, :] = tc[s]
        trow[:, s * 128 : s * 128 + 128] = tc[s].T[0:8]


def point_row(trow, sec):
    return (trow[sec : sec + 1, :].astype(I32) - 1) >> 9


def element_col(tcol, sec, count):
    return jnp.broadcast_to((tcol[:, sec : sec + 1].astype(I32) - 1) & 511, (256, count))


def target_mask(trow, tcol, sec, g):
    at = jnp.where(iota((64, 256), 0) + 64 * g == point_row(trow, sec), 1.0, 0.0).astype(BF16)
    where = jnp.where(iota((256, 512), 1) == element_col(tcol, sec, 512), 1.0, 0.0).astype(BF16)
    return dot(at, where)


def outer_traces(get, mask, trace_table, outs):
    xlo, xhi, ylo, yhi = outs
    keep = [mask[:, x * 256 : x * 256 + 256] < 0.5 for x in range(2)]
    e2 = trace_table[32:64, :]
    for c in range(10):
        w = [jnp.where(keep[x], get(c, x), 0.0) for x in range(2)]
        xlo[0, c] = sum(float(LOW[a]) * w[0][16 * a : 16 * a + 16] for a in range(4))
        xhi[0, c] = sum(float(HIGHV[a]) * w[1][16 * a : 16 * a + 16] for a in range(4))
        for y, out in ((0, ylo), (1, yhi)):
            both = jnp.concatenate([w[x][:, y * 128 : y * 128 + 128] for x in range(2)], axis=1)
            hi, lo = split(both)
            res = dot(e2[16 * y : 16 * y + 16], jnp.concatenate([hi, lo, hi], axis=0))
            out[0, c] = res


def trace_kernel(field, trow, tcol, table, *outs):
    g = pl.program_id(0)
    mask = target_mask(trow, tcol, 0, g)
    outer_traces(lambda c, x: field[c // 5, c % 5, 0, x], mask, table, outs)
    info = jnp.concatenate([trow[0:2, :], jnp.ones((1, 256), F32), jnp.zeros((13, 256), F32)], axis=0)
    for out in outs:
        out[0, 10] = info


def interpolate_part(field_rows, asked, sec, base, picks, first):
    ids = asked[256 + 2 * sec : 256 + 2 * sec + 2, :]
    row = jnp.concatenate([ids[0:1], ids[1:2]], axis=1).astype(I32)
    chosen = jnp.where(iota((256, 256), 0) + base == row, 1.0, 0.0).astype(BF16)
    hi, lo = split(field_rows)
    part = dot(hi, chosen) + dot(lo, chosen)

    @pl.when(first)
    def _():
        picks[...] = part

    @pl.when(jnp.logical_not(first))
    def _():
        picks[...] += part


def answer(asked, sec, picks):
    w = jnp.concatenate([asked[sec * 128 : sec * 128 + 64], asked[sec * 128 + 64 : sec * 128 + 128]], axis=1)
    rows = [jnp.sum(picks[64 * c : 64 * c + 64, :] * w, axis=0, keepdims=True) for c in range(10)]
    value = jnp.concatenate(
        [r[:, 0:128] for r in rows]
        + [jnp.zeros((2, 128), F32)]
        + [r[:, 128:256] for r in rows]
        + [jnp.zeros((2, 128), F32)],
        axis=0,
    )
    groups = [value] + [pltpu.roll(value, by, 1) for by in (16, 112, 1, 127)] + [jnp.zeros((8, 128), F32)]
    return jnp.concatenate(groups, axis=0).T


def interpolate_kernel(field, req, resp, asked, picks):
    g = pl.program_id(0)

    @pl.when(g == 0)
    def _():
        asked[...] = req[...].T

    for x in range(2):
        rows = jnp.concatenate([field[c // 5, c % 5, 0, x] for c in range(10)], axis=0)
        first = (g == 0) if x == 0 else jnp.bool_(False)
        interpolate_part(rows, asked, 0, g * 512 + x * 256, picks, first)

    @pl.when(g == 1)
    def _():
        resp[...] = answer(asked, 0, picks)


def section_kernel(last, *refs):
    it = iter(refs)
    take = lambda n: [next(it) for _ in range(n)]
    (field,) = take(1)
    (first_in,) = take(1) if last else (None,)
    (req,) = take(1) if not last else (None,)
    resp, trow, tcol, main_t, trace_t = take(5)
    halo = take(4)
    info = take(4)
    if last:
        (result,) = take(1)
        (now,) = take(1)
    else:
        now_ref, result, resp_out = take(3)
        halo_out = take(4)
        (now,) = take(1)
    (got, lhs, xl, xr, yl, yr, zl, zr, hx, hy, hz, vol) = take(12)
    if not last:
        asked, picks = take(2)
    g = pl.program_id(0)
    sec = 1 if last else 0

    @pl.when(g == 0)
    def _():
        got[...] = resp[...].T
        if not last:
            asked[...] = req[...].T

    def values(j):
        both = got[24 * j : 24 * j + 24, :]
        return jnp.concatenate([both[0:10], both[12:22]], axis=1)

    val = values(0)
    at = iota((64, 256), 0) + 64 * g == point_row(trow, sec)
    for c in range(10):
        hi, lo = split(jnp.where(at, val[c : c + 1], 0.0))
        lhs[64 * c : 64 * c + 64, 0:256] = hi
        lhs[64 * c : 64 * c + 64, 256:512] = lo
    where = jnp.where(iota((256, 512), 1) == element_col(tcol, sec, 512), 1.0, 0.0).astype(BF16)
    mask = dot(jnp.where(at, 1.0, 0.0).astype(BF16), where)
    for x in range(2):
        wx = where[:, x * 256 : x * 256 + 256]
        scat = dot(lhs[...], jnp.concatenate([wx, wx], axis=0))
        hit = mask[:, x * 256 : x * 256 + 256] > 0.5
        for c in range(10):
            now[c, x] = jnp.where(hit, scat[64 * c : 64 * c + 64], field[c // 5, c % 5, 0, x])

    for c in range(10):
        for x in range(2):
            hi, lo = split(now[c, x])
            res = dot(trace_t[...], jnp.concatenate([hi, lo, hi], axis=0))
            xr[c, x] = res[0:16]
            xl[c, x + 1] = res[16:32]
            yr[c, x, 0] = res[32:48, 0:128]
            yr[c, x, 1] = res[32:48, 128:256]
            yl[c, x, 1] = res[48:64, 0:128]
            yl[c, x, 2] = res[48:64, 128:256]
            zr[c, x] = res[64:80]
            zl[c, x] = res[80:96]

    for j in range(4):
        row2 = info[j][0, 0, sec : sec + 1, :]
        present = info[j][0, 0, 2:3, 0:128] > 0.5
        pt = (row2.astype(I32) - 1) >> 9
        q = pt & 63
        elem = (row2.astype(I32) - 1) & 511
        weights = HIGHV if j % 2 == 0 else LOW
        if j < 2:
            fp, coef = q & 15, pick4(q >> 4, weights)
            want = 1 if j == 0 else 0
            place = jnp.where((elem >> 8) == want, elem & 255, -1)
        else:
            fp, coef = ((q >> 4) << 2) | (q & 3), pick4((q >> 2) & 3, weights)
            want = 1 if j == 2 else 0
            place = jnp.where(((elem >> 7) & 1) == want, ((elem >> 8) << 7) | (elem & 127), -1)
        coef = jnp.where((pt >> 6) == g, coef, 0.0)
        nval = values(1 + j) * coef
        hit = iota((16, 256), 0) == fp
        his, los = [], []
        for c in range(10):
            hi, lo = split(jnp.where(hit, nval[c : c + 1], 0.0))
            his.append(hi)
            los.append(lo)
        left = jnp.concatenate([jnp.concatenate(his, axis=0), jnp.concatenate(los, axis=0)], axis=1)
        pcol = jnp.broadcast_to(place.astype(F32), (128, 256)).T
        pcol = jnp.concatenate([pcol, pcol], axis=1)
        there = jnp.where(iota((256, 256), 1).astype(F32) == pcol, 1.0, 0.0).astype(BF16)
        fix = dot(left, jnp.concatenate([there, there], axis=0))
        for c in range(10):
            for t in range(2):
                lanes = slice(128 * t, 128 * t + 128)
                theirs = halo[j][0, c, :, lanes] + fix[16 * c : 16 * c + 16, lanes]
                if j == 0:
                    xl[c, 0, :, lanes] = jnp.where(present, theirs, xr[c, 0, :, lanes])
                elif j == 1:
                    xr[c, 2, :, lanes] = jnp.where(present, theirs, xl[c, 2, :, lanes])
                elif j == 2:
                    yl[c, t, 0] = jnp.where(present, theirs, yr[c, t, 0])
                else:
                    yr[c, t, 2] = jnp.where(present, theirs, yl[c, t, 2])

    for t in range(2):
        lanes = slice(128 * t, 128 * t + 128)

        @pl.loop(0, 3)
        def _(face):
            left = [xl[c, face, :, lanes] for c in range(10)]
            right = [xr[c, face, :, lanes] for c in range(10)]
            out, _, _ = common(left, right, 0)
            for c in range(10):
                hx[c, face, :, lanes] = out[c]

    @pl.loop(0, 6)
    def _(i):
        x, face = i // 3, i % 3
        left = [yl[c, x, face] for c in range(10)]
        right = [yr[c, x, face] for c in range(10)]
        out, _, _ = common(left, right, 1)
        for c in range(10):
            hy[c, x, face] = out[c].astype(BF16)

    edge = iota((16, 128), 1) == 0
    for t in range(2):
        lanes = slice(128 * t, 128 * t + 128)

        @pl.loop(0, 2)
        def _(x):
            left = [pltpu.roll(zl[c, x, :, lanes], 1, 1) for c in range(10)]
            right = [zr[c, x, :, lanes] for c in range(10)]
            out, fl, fr = common(left, right, 2)
            for c in range(10):
                hz[c, x, 0:16, lanes] = jnp.where(edge, fr[c], out[c]).astype(BF16)
                hz[c, x, 16:32, lanes] = pltpu.roll(jnp.where(edge, fl[c], out[c]), 127, 1).astype(BF16)

    @pl.loop(0, 8)
    def _(i):
        x, q = i // 4, pl.multiple_of((i % 4) * 16, 16)
        for t in range(2):
            lanes = slice(128 * t, 128 * t + 128)
            w = [now[c, x, pl.ds(q, 16), lanes] for c in range(10)]
            u, du = w[:5], w[5:]
            r, v, vv, p = primitive(u)
            dv, dp = tangent(du, r, v, vv)
            for d in range(3):
                f, df = flux(u, du, v, p, dv, dp, d)
                for c in range(10):
                    vol[c, x, pl.ds(64 * d + q, 16), lanes] = (f + df)[c].astype(BF16)

    scale = DT * 0.5 if last else DT
    for c in range(10):
        for x in range(2):
            faces = [hy[c, x, i] for i in range(3)]
            stacked = jnp.concatenate(
                [
                    vol[c, x],
                    jnp.concatenate([faces[0], faces[1]], axis=1),
                    jnp.concatenate([faces[1], faces[2]], axis=1),
                    hz[c, x],
                ],
                axis=0,
            )
            res = dot(main_t[...], stacked)
            low, high = hx[c, x], hx[c, x + 1]
            for a in range(4):
                rows = slice(16 * a, 16 * a + 16)
                lift = float(-scale * LIFT_HI[a]) * high + float(scale * LIFT_LO[a]) * low
                mine = now[c, x, rows]
                if last:
                    base = 0.5 * (mine + first_in[c // 5, c % 5, 0, x, rows])
                else:
                    base = mine
                    now_ref[c // 5, c % 5, 0, x, rows] = mine
                result[c // 5, c % 5, 0, x, rows] = base + (res[rows] + lift)

    if not last:
        for x in range(2):
            rows = jnp.concatenate([result[c // 5, c % 5, 0, x] for c in range(10)], axis=0)
            start = (g == 0) if x == 0 else jnp.bool_(False)
            interpolate_part(rows, asked, 1, g * 512 + x * 256, picks, start)
        outer_traces(
            lambda c, x: result[c // 5, c % 5, 0, x], target_mask(trow, tcol, 1, g), trace_t, halo_out
        )

        @pl.when(g == 1)
        def _():
            resp_out[...] = answer(asked, 1, picks)


FIELD = (2, 5, 2, 2, 64, 256)


def field_spec():
    return pl.BlockSpec((2, 5, 1, 2, 64, 256), lambda g: (0, 0, g, 0, 0, 0))


def whole(shape):
    return pl.BlockSpec(shape, lambda g: (0,) * len(shape))


def halo_spec(comps):
    return pl.BlockSpec((1, comps, 16, 256), lambda g: (g, 0, 0, 0))


def shape(*dims):
    return jax.ShapeDtypeStruct(dims, F32)


def params(mb):
    return pltpu.CompilerParams(dimension_semantics=("arbitrary",), vmem_limit_bytes=mb * 2**20)


def shift(x, axis, up):
    n = lax.axis_size(axis)
    pairs = [(i, i + 1) if up else (i + 1, i) for i in range(n - 1)]
    return lax.ppermute(x, axis, pairs)


def to_neighbours(traces):
    xlo, xhi, ylo, yhi = traces
    return [
        shift(xhi, "rotor", True),
        shift(xlo, "rotor", False),
        shift(yhi, "tower", True),
        shift(ylo, "tower", False),
    ]


def exchange(x):
    return lax.all_to_all(x, AXES, split_axis=0, concat_axis=0, tiled=True)


def section_call(last, scale, field, first, req, resp, trow, tcol, halos, infos):
    main_t = jnp.asarray((scale * MAIN).astype(np.float32), BF16)
    operands = [field] + ([first] if last else [req]) + [resp, trow, tcol, main_t, jnp.asarray(TRACE)]
    specs = [field_spec()] + ([field_spec()] if last else [whole((128, 384))])
    specs += [whole((128, 128)), whole((8, 256)), whole((256, 128)), whole((64, 256)), whole((96, 192))]
    operands += list(halos) + list(infos)
    specs += [halo_spec(10)] * 4 + [pl.BlockSpec((1, 1, 16, 256), lambda g: (0, 10, 0, 0))] * 4
    scratch = [
        pltpu.VMEM((10, 2, 64, 256), F32),
        pltpu.VMEM((128, 128), F32),
        pltpu.VMEM((640, 512), BF16),
        pltpu.VMEM((10, 3, 16, 256), F32),
        pltpu.VMEM((10, 3, 16, 256), F32),
        pltpu.VMEM((10, 2, 3, 16, 128), F32),
        pltpu.VMEM((10, 2, 3, 16, 128), F32),
        pltpu.VMEM((10, 2, 16, 256), F32),
        pltpu.VMEM((10, 2, 16, 256), F32),
        pltpu.VMEM((10, 3, 16, 256), F32),
        pltpu.VMEM((10, 2, 3, 16, 128), BF16),
        pltpu.VMEM((10, 2, 32, 256), BF16),
        pltpu.VMEM((10, 2, 192, 256), BF16),
    ]
    if last:
        out_shape, out_specs = shape(*FIELD), field_spec()
    else:
        out_shape = [shape(*FIELD), shape(*FIELD), shape(128, 128)] + [shape(2, 10, 16, 256)] * 4
        out_specs = [field_spec(), field_spec(), whole((128, 128))] + [halo_spec(10)] * 4
        scratch += [pltpu.VMEM((384, 128), F32), pltpu.VMEM((640, 256), F32)]
    return pl.pallas_call(
        partial(section_kernel, last),
        grid=(2,),
        in_specs=specs,
        out_specs=out_specs,
        out_shape=out_shape,
        scratch_shapes=scratch,
        compiler_params=params(48),
        cost_estimate=pl.CostEstimate(flops=2 * 10**9, bytes_accessed=10**7, transcendentals=0),
        name="section_last" if last else "section_first",
    )(*operands)


def on_device(field, owner, donor, target, weight):
    req, trow, tcol = pl.pallas_call(
        request_kernel,
        out_shape=[shape(128, 384), shape(8, 256), shape(256, 128)],
        compiler_params=pltpu.CompilerParams(vmem_limit_bytes=16 * 2**20),
        name="request",
    )(owner, donor, target, weight)
    req = exchange(req)
    traces = pl.pallas_call(
        trace_kernel,
        grid=(2,),
        in_specs=[field_spec(), whole((8, 256)), whole((256, 128)), whole((96, 192))],
        out_specs=[halo_spec(11)] * 4,
        out_shape=[shape(2, 11, 16, 256)] * 4,
        compiler_params=params(24),
        cost_estimate=pl.CostEstimate(flops=10**8, bytes_accessed=4 * 10**6, transcendentals=0),
        name="traces",
    )(field, trow, tcol, jnp.asarray(TRACE))
    infos = to_neighbours(traces)
    resp = pl.pallas_call(
        interpolate_kernel,
        grid=(2,),
        in_specs=[field_spec(), whole((128, 384))],
        out_specs=whole((128, 128)),
        out_shape=shape(128, 128),
        scratch_shapes=[pltpu.VMEM((384, 128), F32), pltpu.VMEM((640, 256), F32)],
        compiler_params=params(24),
        cost_estimate=pl.CostEstimate(flops=10**9, bytes_accessed=4 * 10**6, transcendentals=0),
        name="interpolate",
    )(field, req)
    resp = exchange(resp)
    first, middle, resp, *traces = section_call(
        False, -DT, field, None, req, resp, trow, tcol, infos, infos
    )
    halos = to_neighbours(traces)
    resp = exchange(resp)
    return section_call(True, -0.5 * DT, middle, first, None, resp, trow, tcol, halos, infos)


def solution(mesh):
    placed = (
        P(None, None, None, "rotor", None, "tower"),
        P("rotor", "tower", None, None, None),
        P("rotor", "tower", None, None),
        P("rotor", "tower", None, None),
        P("rotor", "tower", None, None, None),
    )
    return jax.shard_map(
        on_device,
        mesh=mesh,
        in_specs=placed,
        out_specs=P(None, None, None, "rotor", None, "tower"),
        check_vma=False,
    )
```

profile of v0, /device:TPU:1, one launch (start us, length us, event | category | flops | bytes accessed | tf_op | source)
XLA Modules:
  0.0 112.9 jit_solution(10439129496555862957)
XLA Ops:
  0.0 0.8 copy.11.owner
  0.8 0.9 copy.12.weight
  1.8 0.0 copy-start.7
  1.8 0.7 copy-done.7
  2.4 0.0 copy-start.8
  2.4 0.7 copy-done.8
  3.1 0.8 request.1
  3.9 0.0 copy-start
  3.9 1.7 %copy-done = f32[2,5,2,2,64,256]{5,4,3,2,1,0:T(8,128)S(1)} copy-done((f32[2,5,2,2,64,256]{5,4,3,2,1,0:T(8,128)S(1)}, f32[2,5,2,2,64,256]{5,4,3,2,1,0:T(8,128)}, u32[]{:S(2)}) %copy-start) | copy-done | bytes 2621464
  5.6 0.0 copy-start.4
  5.6 0.8 copy-done.4
  6.4 0.0 copy-start.1
  6.4 1.6 %traces.1 = (f32[2,11,16,256]{3,2,1,0:T(8,128)S(1)}, f32[2,11,16,256]{3,2,1,0:T(8,128)S(1)}, f32[2,11,16,256]{3,2,1,0:T(8,128)S(1)}, f32[2,11,16,256]{3,2,1,0:T(8,128)S(1)}) custom-call(f32[2,5,2,2,64,256]{5,4,3,2,1,0:T(8,128)S(1)} %copy-done, f32[8,256]{1,0:T(8,128)S(1)} %get-tuple-element.20.trow.refs_3_, f32[256,128]{1,0:T(8,128)S(1)} %get-tuple-element.21.tcol.refs_4_, ...), custom_call_target="tpu_custom_call" | custom-call | flops 100000000 | bytes 4000000 | tf_op jit(solution)/shard_map/traces/pallas_call | solution.py:547
  8.0 0.0 copy-start.5
  8.0 0.0 copy-start.9
  8.0 4.7 %collective-permute-start = (f32[2,11,16,256]{3,2,1,0:T(8,128)S(1)}, f32[2,11,16,256]{3,2,1,0:T(8,128)S(1)}, u32[]{:S(2)}, u32[]{:S(2)}) collective-permute-start(f32[2,11,16,256]{3,2,1,0:T(8,128)S(1)} %get-tuple-element.22), channel_id=1, source_target_pairs={{0,16},{16,32},{32,48},{48,64},{64,80},{80,96},{96,112},{1,17},{17... | collective-permute-start | bytes 1081352 | tf_op jit(solution)/shard_map/ppermute | solution.py:481
  12.8 1.9 %collective-permute-start.1 = (f32[2,11,16,256]{3,2,1,0:T(8,128)S(1)}, f32[2,11,16,256]{3,2,1,0:T(8,128)S(1)}, u32[]{:S(2)}, u32[]{:S(2)}) collective-permute-start(f32[2,11,16,256]{3,2,1,0:T(8,128)S(1)} %get-tuple-element.23), channel_id=1, source_target_pairs={{16,0},{32,16},{48,32},{64,48},{80,64},{96,80},{112,96},{17,1},{33... | collective-permute-start | bytes 1081352 | tf_op jit(solution)/shard_map/ppermute | solution.py:481
  14.7 3.1 %collective-permute-start.2 = (f32[2,11,16,256]{3,2,1,0:T(8,128)S(1)}, f32[2,11,16,256]{3,2,1,0:T(8,128)S(1)}, u32[]{:S(2)}, u32[]{:S(2)}) collective-permute-start(f32[2,11,16,256]{3,2,1,0:T(8,128)S(1)} %get-tuple-element.24), channel_id=1, source_target_pairs={{0,1},{1,2},{2,3},{3,4},{4,5},{5,6},{6,7},{7,8},{8,9},{9,10},{10,1... | collective-permute-start | bytes 1081352 | tf_op jit(solution)/shard_map/ppermute | solution.py:481
  17.8 1.3 %collective-permute-start.3 = (f32[2,11,16,256]{3,2,1,0:T(8,128)S(1)}, f32[2,11,16,256]{3,2,1,0:T(8,128)S(1)}, u32[]{:S(2)}, u32[]{:S(2)}) collective-permute-start(f32[2,11,16,256]{3,2,1,0:T(8,128)S(1)} %get-tuple-element.25), channel_id=1, source_target_pairs={{1,0},{2,1},{3,2},{4,3},{5,4},{6,5},{7,6},{8,7},{9,8},{10,9},{11,1... | collective-permute-start | bytes 1081352 | tf_op jit(solution)/shard_map/ppermute | solution.py:481
  19.1 0.2 copy.13
  19.4 22.6 %all_to_all.33 = f32[128,1,384]{2,1,0:T(1,128)S(1)} all-to-all(f32[128,1,384]{2,1,0:T(1,128)S(1)} %copy.13), channel_id=1, replica_groups=mesh['rotor'=8,'tower'=16] {'rotor','tower'}, dimensions={0} | all-to-all | bytes 393216 | tf_op jit(solution)/shard_map/all_to_all | solution.py:495
  41.9 0.0 copy-done.1
  42.0 2.6 %interpolate.1 = f32[128,128]{1,0:T(8,128)S(1)} custom-call(f32[2,5,2,2,64,256]{5,4,3,2,1,0:T(8,128)S(1)} %copy-done.1, f32[128,384]{1,0:T(8,128)S(1)} %bitcast.13), custom_call_target="tpu_custom_call" | custom-call | flops 1000000000 | bytes 4000000 | tf_op jit(solution)/shard_map/interpolate/pallas_call | solution.py:558
  44.6 13.6 %all_to_all.34 = f32[128,1,128]{2,1,0:T(1,128)S(1)} all-to-all(f32[128,1,128]{2,1,0:T(1,128)S(1)} %bitcast.18), channel_id=1, replica_groups=mesh['rotor'=8,'tower'=16] {'rotor','tower'}, dimensions={0} | all-to-all | bytes 131072 | tf_op jit(solution)/shard_map/all_to_all | solution.py:495
  58.2 0.0 collective-permute-done.refs_7_.refs_11_
  58.2 0.0 collective-permute-done.1.refs_8_.refs_12_
  58.2 0.0 collective-permute-done.2.refs_9_.refs_13_
  58.2 0.0 collective-permute-done.3.refs_10_.refs_14_
  58.2 0.0 copy-done.5
  58.2 0.0 copy-done.9
  58.2 0.0 copy-start.6
  58.2 13.8 %section_first.1 = (f32[2,5,2,2,64,256]{5,4,3,2,1,0:T(8,128)S(1)}, f32[2,5,2,2,64,256]{5,4,3,2,1,0:T(8,128)}, f32[128,128]{1,0:T(8,128)S(1)}, f32[2,10,16,256]{3...) custom-call(f32[2,5,2,2,64,256]{5,4,3,2,1,0:T(8,128)} %refs_0_.1, ...), custom_call_target="tpu_custom_call" | custom-call | flops 2000000000 | bytes 10000000 | tf_op jit(solution)/shard_map/section_first/pallas_call | solution.py:526
  72.1 0.0 copy-start.2
  72.1 1.5 %copy-done.2 = f32[2,5,2,2,64,256]{5,4,3,2,1,0:T(8,128)} copy-done((f32[2,5,2,2,64,256]{5,4,3,2,1,0:T(8,128)}, f32[2,5,2,2,64,256]{5,4,3,2,1,0:T(8,128)S(1)}, u32[]{:S(2)}) %copy-start.2) | copy-done | bytes 2621464
  73.6 2.9 %collective-permute-start.4 = (f32[2,10,16,256]{3,2,1,0:T(8,128)S(1)}, f32[2,10,16,256]{3,2,1,0:T(8,128)S(1)}, u32[]{:S(2)}, u32[]{:S(2)}) collective-permute-start(f32[2,10,16,256]{3,2,1,0:T(8,128)S(1)} %get-tuple-element.29), channel_id=1, source_target_pairs={{0,16},{16,32},{32,48},{48,64},{64,80},{80,96},{96,112},{1,17},{17... | collective-permute-start | bytes 983048 | tf_op jit(solution)/shard_map/ppermute | solution.py:481
  76.5 1.9 %collective-permute-start.5 = (f32[2,10,16,256]{3,2,1,0:T(8,128)S(1)}, f32[2,10,16,256]{3,2,1,0:T(8,128)S(1)}, u32[]{:S(2)}, u32[]{:S(2)}) collective-permute-start(f32[2,10,16,256]{3,2,1,0:T(8,128)S(1)} %get-tuple-element.30), channel_id=1, source_target_pairs={{16,0},{32,16},{48,32},{64,48},{80,64},{96,80},{112,96},{17,1},{33... | collective-permute-start | bytes 983048 | tf_op jit(solution)/shard_map/ppermute | solution.py:481
  78.4 2.2 %collective-permute-start.6 = (f32[2,10,16,256]{3,2,1,0:T(8,128)S(1)}, f32[2,10,16,256]{3,2,1,0:T(8,128)S(1)}, u32[]{:S(2)}, u32[]{:S(2)}) collective-permute-start(f32[2,10,16,256]{3,2,1,0:T(8,128)S(1)} %get-tuple-element.31), channel_id=1, source_target_pairs={{0,1},{1,2},{2,3},{3,4},{4,5},{5,6},{6,7},{7,8},{8,9},{9,10},{10,1... | collective-permute-start | bytes 983048 | tf_op jit(solution)/shard_map/ppermute | solution.py:481
  80.6 1.3 %collective-permute-start.7 = (f32[2,10,16,256]{3,2,1,0:T(8,128)S(1)}, f32[2,10,16,256]{3,2,1,0:T(8,128)S(1)}, u32[]{:S(2)}, u32[]{:S(2)}) collective-permute-start(f32[2,10,16,256]{3,2,1,0:T(8,128)S(1)} %get-tuple-element.32), channel_id=1, source_target_pairs={{1,0},{2,1},{3,2},{4,3},{5,4},{6,5},{7,6},{8,7},{9,8},{10,9},{11,1... | collective-permute-start | bytes 983048 | tf_op jit(solution)/shard_map/ppermute | solution.py:481
  81.9 18.3 %all_to_all.35 = f32[128,1,128]{2,1,0:T(1,128)S(1)} all-to-all(f32[128,1,128]{2,1,0:T(1,128)S(1)} %bitcast.17), channel_id=1, replica_groups=mesh['rotor'=8,'tower'=16] {'rotor','tower'}, dimensions={0} | all-to-all | bytes 131072 | tf_op jit(solution)/shard_map/all_to_all | solution.py:495
  100.3 0.0 collective-permute-done.4.refs_7_
  100.3 0.0 collective-permute-done.5.refs_8_
  100.3 0.0 collective-permute-done.6.refs_9_
  100.3 0.0 collective-permute-done.7.refs_10_
  100.3 0.0 copy-done.6
  100.3 0.0 copy-start.3
  100.3 1.7 %copy-done.3 = f32[2,5,2,2,64,256]{5,4,3,2,1,0:T(8,128)S(1)} copy-done((f32[2,5,2,2,64,256]{5,4,3,2,1,0:T(8,128)S(1)}, f32[2,5,2,2,64,256]{5,4,3,2,1,0:T(8,128)}, u32[]{:S(2)}) %copy-start.3) | copy-done | bytes 2621464
  102.0 10.8 %section_last.1 = f32[2,5,2,2,64,256]{5,4,3,2,1,0:T(8,128)} custom-call(f32[2,5,2,2,64,256]{5,4,3,2,1,0:T(8,128)S(1)} %copy-done.3, f32[2,5,2,2,64,256]{5,4,3,2,1,0:T(8,128)} %copy-done.2, f32[128,128]{1,0:T(8,128)S(1)} %bitcast.12, f32[8,256]{1,0:T(8,128)S(1)} %get-tuple-element.20.trow.refs_3_, f32[256,128]{1,0:T(8,128)S(1)} %get-tuple-element.21.tcol.refs_4_, ...), custom_call_target="tpu_custom_call" | custom-call | flops 2000000000 | bytes 10000000 | tf_op jit(solution)/shard_map/section_last/pallas_call | solution.py:526
  (1 shorter events, 0.0 us)
Async XLA Ops:
  1.8 0.7 copy-start.7
  2.4 0.7 copy-start.8
  3.9 1.7 %copy-start = (f32[2,5,2,2,64,256]{5,4,3,2,1,0:T(8,128)S(1)}, f32[2,5,2,2,64,256]{5,4,3,2,1,0:T(8,128)}, u32[]{:S(2)}) copy-start(f32[2,5,2,2,64,256]{5,4,3,2,1,0:T(8,128)} %refs_0_.1) | copy-start | bytes 7864324
  5.6 0.8 copy-start.4
  6.4 35.5 %copy-start.1 = (f32[2,5,2,2,64,256]{5,4,3,2,1,0:T(8,128)S(1)}, f32[2,5,2,2,64,256]{5,4,3,2,1,0:T(8,128)}, u32[]{:S(2)}) copy-start(f32[2,5,2,2,64,256]{5,4,3,2,1,0:T(8,128)} %refs_0_.1) | copy-start | bytes 7864324
  8.0 50.2 %copy-start.5 = (bf16[96,192]{1,0:T(8,128)(2,1)S(1)}, bf16[96,192]{1,0:T(8,128)(2,1)}, u32[]{:S(2)}) copy-start(bf16[96,192]{1,0:T(8,128)(2,1)} %constant.6.clone.table.refs_6_) | copy-start | bytes 110596
  8.0 50.2 %copy-start.9 = (bf16[64,256]{1,0:T(8,128)(2,1)S(1)}, bf16[64,256]{1,0:T(8,128)(2,1)}, u32[]{:S(2)}) copy-start(bf16[64,256]{1,0:T(8,128)(2,1)} %constant.7.clone.refs_5_) | copy-start | bytes 98308
  8.0 50.2 %collective-permute-start = (f32[2,11,16,256]{3,2,1,0:T(8,128)S(1)}, f32[2,11,16,256]{3,2,1,0:T(8,128)S(1)}, u32[]{:S(2)}, u32[]{:S(2)}) collective-permute-start(f32[2,11,16,256]{3,2,1,0:T(8,128)S(1)} %get-tuple-element.22), channel_id=1, source_target_pairs={{0,16},{16,32},{32,48},{48,64},{64,80},{80,96},{96,112},{1,17},{17... | collective-permute-start | bytes 1081352 | tf_op jit(solution)/shard_map/ppermute | solution.py:481
  12.8 45.4 %collective-permute-start.1 = (f32[2,11,16,256]{3,2,1,0:T(8,128)S(1)}, f32[2,11,16,256]{3,2,1,0:T(8,128)S(1)}, u32[]{:S(2)}, u32[]{:S(2)}) collective-permute-start(f32[2,11,16,256]{3,2,1,0:T(8,128)S(1)} %get-tuple-element.23), channel_id=1, source_target_pairs={{16,0},{32,16},{48,32},{64,48},{80,64},{96,80},{112,96},{17,1},{33... | collective-permute-start | bytes 1081352 | tf_op jit(solution)/shard_map/ppermute | solution.py:481
  14.7 43.5 %collective-permute-start.2 = (f32[2,11,16,256]{3,2,1,0:T(8,128)S(1)}, f32[2,11,16,256]{3,2,1,0:T(8,128)S(1)}, u32[]{:S(2)}, u32[]{:S(2)}) collective-permute-start(f32[2,11,16,256]{3,2,1,0:T(8,128)S(1)} %get-tuple-element.24), channel_id=1, source_target_pairs={{0,1},{1,2},{2,3},{3,4},{4,5},{5,6},{6,7},{7,8},{8,9},{9,10},{10,1... | collective-permute-start | bytes 1081352 | tf_op jit(solution)/shard_map/ppermute | solution.py:481
  17.8 40.4 %collective-permute-start.3 = (f32[2,11,16,256]{3,2,1,0:T(8,128)S(1)}, f32[2,11,16,256]{3,2,1,0:T(8,128)S(1)}, u32[]{:S(2)}, u32[]{:S(2)}) collective-permute-start(f32[2,11,16,256]{3,2,1,0:T(8,128)S(1)} %get-tuple-element.25), channel_id=1, source_target_pairs={{1,0},{2,1},{3,2},{4,3},{5,4},{6,5},{7,6},{8,7},{9,8},{10,9},{11,1... | collective-permute-start | bytes 1081352 | tf_op jit(solution)/shard_map/ppermute | solution.py:481
  58.2 42.0 %copy-start.6 = (bf16[64,256]{1,0:T(8,128)(2,1)S(1)}, bf16[64,256]{1,0:T(8,128)(2,1)}, u32[]{:S(2)}) copy-start(bf16[64,256]{1,0:T(8,128)(2,1)} %constant.8.clone.refs_5_) | copy-start | bytes 98308
  72.1 1.5 %copy-start.2 = (f32[2,5,2,2,64,256]{5,4,3,2,1,0:T(8,128)}, f32[2,5,2,2,64,256]{5,4,3,2,1,0:T(8,128)S(1)}, u32[]{:S(2)}) copy-start(f32[2,5,2,2,64,256]{5,4,3,2,1,0:T(8,128)S(1)} %get-tuple-element.27.refs_1_) | copy-start | bytes 7864324
  73.6 26.7 %collective-permute-start.4 = (f32[2,10,16,256]{3,2,1,0:T(8,128)S(1)}, f32[2,10,16,256]{3,2,1,0:T(8,128)S(1)}, u32[]{:S(2)}, u32[]{:S(2)}) collective-permute-start(f32[2,10,16,256]{3,2,1,0:T(8,128)S(1)} %get-tuple-element.29), channel_id=1, source_target_pairs={{0,16},{16,32},{32,48},{48,64},{64,80},{80,96},{96,112},{1,17},{17... | collective-permute-start | bytes 983048 | tf_op jit(solution)/shard_map/ppermute | solution.py:481
  76.5 23.8 %collective-permute-start.5 = (f32[2,10,16,256]{3,2,1,0:T(8,128)S(1)}, f32[2,10,16,256]{3,2,1,0:T(8,128)S(1)}, u32[]{:S(2)}, u32[]{:S(2)}) collective-permute-start(f32[2,10,16,256]{3,2,1,0:T(8,128)S(1)} %get-tuple-element.30), channel_id=1, source_target_pairs={{16,0},{32,16},{48,32},{64,48},{80,64},{96,80},{112,96},{17,1},{33... | collective-permute-start | bytes 983048 | tf_op jit(solution)/shard_map/ppermute | solution.py:481
  78.4 21.9 %collective-permute-start.6 = (f32[2,10,16,256]{3,2,1,0:T(8,128)S(1)}, f32[2,10,16,256]{3,2,1,0:T(8,128)S(1)}, u32[]{:S(2)}, u32[]{:S(2)}) collective-permute-start(f32[2,10,16,256]{3,2,1,0:T(8,128)S(1)} %get-tuple-element.31), channel_id=1, source_target_pairs={{0,1},{1,2},{2,3},{3,4},{4,5},{5,6},{6,7},{7,8},{8,9},{9,10},{10,1... | collective-permute-start | bytes 983048 | tf_op jit(solution)/shard_map/ppermute | solution.py:481
  80.6 19.6 %collective-permute-start.7 = (f32[2,10,16,256]{3,2,1,0:T(8,128)S(1)}, f32[2,10,16,256]{3,2,1,0:T(8,128)S(1)}, u32[]{:S(2)}, u32[]{:S(2)}) collective-permute-start(f32[2,10,16,256]{3,2,1,0:T(8,128)S(1)} %get-tuple-element.32), channel_id=1, source_target_pairs={{1,0},{2,1},{3,2},{4,3},{5,4},{6,5},{7,6},{8,7},{9,8},{10,9},{11,1... | collective-permute-start | bytes 983048 | tf_op jit(solution)/shard_map/ppermute | solution.py:481
  100.3 1.7 %copy-start.3 = (f32[2,5,2,2,64,256]{5,4,3,2,1,0:T(8,128)S(1)}, f32[2,5,2,2,64,256]{5,4,3,2,1,0:T(8,128)}, u32[]{:S(2)}) copy-start(f32[2,5,2,2,64,256]{5,4,3,2,1,0:T(8,128)} %get-tuple-element.26.refs_0_) | copy-start | bytes 7864324
where the time goes:
time: 114 us; the launch traced here: 113 us
  blocking collectives  54.5 us (48%)
  Pallas kernels  29.6 us (26%)
  starting transfers between devices  19.4 us (17%)
  local copies, waits for them, and re-layouts  9.1 us (8%)
    all_to_all x3, blocking collectives, exchange(): return lax.all_to_all(x, AXES, split_axis=0, concat_axis=0, tiled=True)  54.5 us
    pallas_call x2, Pallas kernels, section_call(): pl.pallas_call(partial(section_kernel, last), grid=(2,), in_specs=specs,...  24.6 us
    ppermute x8, starting transfers between devices, shift(): return lax.ppermute(x, axis, pairs)  19.4 us
    unnamed x23, local copies, waits for them, and re-layouts  8.9 us
    pallas_call x1, Pallas kernels, on_device(): pl.pallas_call(interpolate_kernel, grid=(2,), in_specs=[field_spec(), who...  2.64 us
  transfers between devices with their start and end apart: 8, of which 0 were waited for; matrix products, arithmetic and copies ran while one was open for 0% of the time, Pallas kernels for 2%

commit v1 on v0

v1 whole, which is shorter than its diff:
```python
from functools import partial

import jax
import jax.numpy as jnp
import numpy as np
from jax import lax
from jax.experimental import pallas as pl
from jax.experimental.pallas import tpu as pltpu
from jax.sharding import PartitionSpec as P

DT = 0.01
DEV = 128
AXES = ("rotor", "tower")
F32, BF16, I32 = jnp.float32, jnp.bfloat16, jnp.int32
HIGH = lax.Precision.HIGHEST


def lagrange_values(nodes, at):
    values = np.ones(4)
    for j in range(4):
        for m in range(4):
            if m != j:
                values[j] *= (at - nodes[m]) / (nodes[j] - nodes[m])
    return values


def lagrange_slopes(nodes, at):
    slopes = np.zeros(4)
    for j in range(4):
        for k in range(4):
            if k != j:
                factor = 1.0 / (nodes[j] - nodes[k])
                for m in range(4):
                    if m != j and m != k:
                        factor *= (at - nodes[m]) / (nodes[j] - nodes[m])
                slopes[j] += factor
    return slopes


def expand(block, axis):
    pieces = [np.eye(4)] * 3
    pieces[axis] = block
    return np.kron(np.kron(pieces[0], pieces[1]), pieces[2])


NODES = np.array([-0.8611363115940526, -0.3399810435848563, 0.3399810435848563, 0.8611363115940526])
QUAD = np.array([0.3478548451374538, 0.6521451548625461, 0.6521451548625461, 0.3478548451374538])
SLOPES = np.stack([lagrange_slopes(NODES, at) for at in NODES])
LOW, HIGHV = lagrange_values(NODES, -1.0), lagrange_values(NODES, 1.0)
LIFT_LO, LIFT_HI = LOW / QUAD, HIGHV / QUAD


def halves(table):
    hi = table.astype(np.float32).astype(jnp.bfloat16)
    lo = (table - hi.astype(np.float64)).astype(jnp.bfloat16)
    return hi, lo


def tables():
    e_lo = [expand(LOW[None, :], d) for d in range(3)]
    e_hi = [expand(HIGHV[None, :], d) for d in range(3)]
    l_lo = [expand(LIFT_LO[:, None], d) for d in range(3)]
    l_hi = [expand(LIFT_HI[:, None], d) for d in range(3)]
    weak = [expand(SLOPES, d) - l_hi[d] @ e_hi[d] + l_lo[d] @ e_lo[d] for d in range(3)]
    main = np.concatenate(weak + [-l_lo[2], l_hi[2], -l_lo[1], l_hi[1]], axis=1)
    trace = np.concatenate([t for d in range(3) for t in (e_lo[d], e_hi[d])], axis=0)
    t_hi, t_lo = halves(trace)
    return main, np.concatenate([t_hi, t_hi, t_lo], axis=1)


MAIN, TRACE = tables()


def iota(shape, dim):
    return lax.broadcasted_iota(I32, shape, dim)


def dot(a, b, precision=None):
    return lax.dot_general(a, b, (((1,), (0,)), ((), ())), precision=precision, preferred_element_type=F32)


def split(x):
    hi = x.astype(BF16)
    return hi, (x - hi.astype(F32)).astype(BF16)


def pick4(index, values):
    out = jnp.full(index.shape, float(values[3]), F32)
    for i in range(3):
        out = jnp.where(index == i, float(values[i]), out)
    return out


def primitive(u):
    rho, m1, m2, m3, en = u
    r = 1.0 / rho
    v = [m1 * r, m2 * r, m3 * r]
    vv = v[0] * v[0] + v[1] * v[1] + v[2] * v[2]
    p = 0.4 * (en - 0.5 * rho * vv)
    return r, v, vv, p


def tangent(du, r, v, vv):
    dv = [(du[1 + i] - v[i] * du[0]) * r for i in range(3)]
    dp = 0.4 * (du[4] - (v[0] * du[1] + v[1] * du[2] + v[2] * du[3]) + 0.5 * vv * du[0])
    return dv, dp


def flux(u, du, v, p, dv, dp, d):
    out = [u[1 + d]]
    dout = [du[1 + d]]
    for i in range(3):
        f = u[1 + i] * v[d]
        df = du[1 + i] * v[d] + u[1 + i] * dv[d]
        if i == d:
            f, df = f + (p - 1.0), df + dp
        out.append(f)
        dout.append(df)
    out.append((u[4] + p) * v[d])
    dout.append((du[4] + dp) * v[d] + (u[4] + p) * dv[d])
    return out, dout


def side(w, d):
    u, du = w[:5], w[5:]
    r, v, vv, p = primitive(u)
    dv, dp = tangent(du, r, v, vv)
    f, df = flux(u, du, v, p, dv, dp, d)
    c2 = 1.4 * p * r
    dc2 = 1.4 * r * dp - c2 * r * du[0]
    s2 = v[d] * v[d] + c2
    r1, r2 = lax.rsqrt(c2), lax.rsqrt(s2)
    s = c2 * r1 + s2 * r2
    ds = 0.5 * dc2 * r1 + (v[d] * dv[d] + 0.5 * dc2) * r2
    return f + df, s, ds


def common(left, right, d):
    fl, sl, dsl = side(left, d)
    fr, sr, dsr = side(right, d)
    s, ds = 0.25 * (sl + sr), 0.25 * (dsl + dsr)
    out = []
    for i in range(5):
        out.append(0.5 * (fl[i] + fr[i]) - s * (right[i] - left[i]))
    for i in range(5):
        out.append(
            0.5 * (fl[5 + i] + fr[5 + i]) - ds * (right[i] - left[i]) - s * (right[5 + i] - left[5 + i])
        )
    return out, fl, fr


def request_kernel(owner, donor, target, weight, req, trow, tcol):
    sub, lane = iota((DEV, DEV), 0), iota((DEV, DEV), 1)
    results = []
    tc = [jnp.zeros((DEV, DEV), F32) for _ in range(2)]
    for sec in range(2):
        orow = jnp.broadcast_to(owner[sec : sec + 1].astype(F32), (DEV, DEV))
        oc = orow.T
        same = (oc == orow) & (sub < lane)
        pos = jnp.sum(jnp.where(same, 1.0, 0.0), axis=0, keepdims=True)
        lists = [weight[sec], donor[sec : sec + 1].astype(F32), target[sec : sec + 1].astype(F32) + 1.0]
        rhs = jnp.concatenate(lists + [jnp.zeros((62, DEV), F32)], axis=0).T
        for s in range(2):
            chosen = (orow == sub.astype(F32)) & (pos == float(s))
            res = dot(jnp.where(chosen, 1.0, 0.0), rhs, HIGH)
            results.append(res)
            tc[s] = jnp.where(lane == sec, res[:, 65:66], tc[s])
    for sec in range(2):
        pair = jnp.where(lane < 64, results[2 * sec], pltpu.roll(results[2 * sec + 1], 64, 1))
        req[pl.ds(sec, DEV, stride=3), :] = pair
    ids = jnp.zeros((DEV, DEV), F32)
    for i in range(4):
        ids = jnp.where(lane == i, results[i][:, 64:65], ids)
    req[pl.ds(2, DEV, stride=3), :] = ids
    for s in range(2):
        tcol[s * 128 : s * 128 + 128, :] = tc[s]
        trow[:, s * 128 : s * 128 + 128] = tc[s].T[0:8]


def point_row(trow, sec):
    return (trow[sec : sec + 1, :].astype(I32) - 1) >> 9


def element_col(tcol, sec, count):
    return jnp.broadcast_to((tcol[:, sec : sec + 1].astype(I32) - 1) & 511, (256, count))


def target_mask(trow, tcol, sec, g):
    at = jnp.where(iota((64, 256), 0) + 64 * g == point_row(trow, sec), 1.0, 0.0).astype(BF16)
    where = jnp.where(iota((256, 512), 1) == element_col(tcol, sec, 512), 1.0, 0.0).astype(BF16)
    return dot(at, where)


def outer_traces(get, mask, trace_table, outs):
    xlo, xhi, ylo, yhi = outs
    keep = [mask[:, x * 256 : x * 256 + 256] < 0.5 for x in range(2)]
    e2 = trace_table[32:64, :]
    for c in range(10):
        w = [jnp.where(keep[x], get(c, x), 0.0) for x in range(2)]
        xlo[0, c] = sum(float(LOW[a]) * w[0][16 * a : 16 * a + 16] for a in range(4))
        xhi[0, c] = sum(float(HIGHV[a]) * w[1][16 * a : 16 * a + 16] for a in range(4))
        for y, out in ((0, ylo), (1, yhi)):
            both = jnp.concatenate([w[x][:, y * 128 : y * 128 + 128] for x in range(2)], axis=1)
            hi, lo = split(both)
            res = dot(e2[16 * y : 16 * y + 16], jnp.concatenate([hi, lo, hi], axis=0))
            out[0, c] = res


def trace_kernel(sec, field, trow, tcol, table, *outs):
    g = pl.program_id(0)
    mask = target_mask(trow, tcol, sec, g)
    outer_traces(lambda c, x: field[c // 5, c % 5, 0, x], mask, table, outs)
    if sec == 1:
        return
    info = jnp.concatenate([trow[0:2, :], jnp.ones((1, 256), F32), jnp.zeros((13, 256), F32)], axis=0)
    for out in outs:
        out[0, 10] = info


def load_asked(req, asked):
    for i in range(3):
        asked[i * 128 : i * 128 + 128, :] = req[pl.ds(i, DEV, stride=3), :].T


def interpolate_part(field_rows, asked, sec, base, picks, first):
    ids = asked[256 + 2 * sec : 256 + 2 * sec + 2, :]
    row = jnp.concatenate([ids[0:1], ids[1:2]], axis=1).astype(I32)
    chosen = jnp.where(iota((256, 256), 0) + base == row, 1.0, 0.0).astype(BF16)
    part = dot(field_rows.astype(BF16), chosen)

    @pl.when(first)
    def _():
        picks[...] = part

    @pl.when(jnp.logical_not(first))
    def _():
        picks[...] += part


def answer(asked, sec, picks):
    w = jnp.concatenate([asked[sec * 128 : sec * 128 + 64], asked[sec * 128 + 64 : sec * 128 + 128]], axis=1)
    rows = [jnp.sum(picks[64 * c : 64 * c + 64, :] * w, axis=0, keepdims=True) for c in range(10)]
    value = jnp.concatenate(
        [r[:, 0:128] for r in rows]
        + [jnp.zeros((2, 128), F32)]
        + [r[:, 128:256] for r in rows]
        + [jnp.zeros((2, 128), F32)],
        axis=0,
    )
    groups = [value] + [pltpu.roll(value, by, 1) for by in (16, 112, 1, 127)] + [jnp.zeros((8, 128), F32)]
    return jnp.concatenate(groups, axis=0).T


def interpolate_kernel(field, req, resp, asked, picks):
    i = pl.program_id(0)

    @pl.when(i == 0)
    def _():
        load_asked(req, asked)

    rows = jnp.concatenate([field[c // 5, c % 5, 0, 0] for c in range(10)], axis=0)
    interpolate_part(rows, asked, 0, i * 256, picks, i == 0)

    @pl.when(i == 3)
    def _():
        resp[...] = answer(asked, 0, picks)


def values(got, j):
    both = got[24 * j : 24 * j + 24, :]
    return jnp.concatenate([both[0:10], both[12:22]], axis=1)


def set_fringe(field, got, trow, tcol, sec, g, lhs, now):
    val = values(got, 0)
    at = iota((64, 256), 0) + 64 * g == point_row(trow, sec)
    for c in range(10):
        hi, lo = split(jnp.where(at, val[c : c + 1], 0.0))
        lhs[64 * c : 64 * c + 64, 0:256] = hi
        lhs[64 * c : 64 * c + 64, 256:512] = lo
    where = jnp.where(iota((256, 512), 1) == element_col(tcol, sec, 512), 1.0, 0.0).astype(BF16)
    mask = dot(jnp.where(at, 1.0, 0.0).astype(BF16), where)
    for x in range(2):
        wx = where[:, x * 256 : x * 256 + 256]
        scat = dot(lhs[...], jnp.concatenate([wx, wx], axis=0))
        hit = mask[:, x * 256 : x * 256 + 256] > 0.5
        for c in range(10):
            now[c, x] = jnp.where(hit, scat[64 * c : 64 * c + 64], field[c // 5, c % 5, 0, x])


def all_traces(now, table, xt, yt, zt):
    for c in range(10):
        for x in range(2):
            hi, lo = split(now[c, x])
            res = dot(table[...], jnp.concatenate([hi, lo, hi], axis=0))
            xt[c, x] = res[0:32]
            yt[c, x] = res[32:64]
            zt[c, x] = res[64:96]


def mend_halos(halo, info, got, sec, g, xt, yt, hal):
    for j in range(4):
        row2 = info[j][0, 0, sec : sec + 1, :]
        present = info[j][0, 0, 2:3, 0:128] > 0.5
        pt = (row2.astype(I32) - 1) >> 9
        q = pt & 63
        elem = (row2.astype(I32) - 1) & 511
        weights = HIGHV if j % 2 == 0 else LOW
        if j < 2:
            fp, coef = q & 15, pick4(q >> 4, weights)
            want = 1 if j == 0 else 0
            place = jnp.where((elem >> 8) == want, elem & 255, -1)
        else:
            fp, coef = ((q >> 4) << 2) | (q & 3), pick4((q >> 2) & 3, weights)
            want = 1 if j == 2 else 0
            place = jnp.where(((elem >> 7) & 1) == want, ((elem >> 8) << 7) | (elem & 127), -1)
        coef = jnp.where((pt >> 6) == g, coef, 0.0)
        nval = values(got, 1 + j) * coef
        hit = iota((16, 256), 0) == fp
        his, los = [], []
        for c in range(10):
            hi, lo = split(jnp.where(hit, nval[c : c + 1], 0.0))
            his.append(hi)
            los.append(lo)
        left = jnp.concatenate([jnp.concatenate(his, axis=0), jnp.concatenate(los, axis=0)], axis=1)
        pcol = jnp.broadcast_to(place.astype(F32), (128, 256)).T
        pcol = jnp.concatenate([pcol, pcol], axis=1)
        there = jnp.where(iota((256, 256), 1).astype(F32) == pcol, 1.0, 0.0).astype(BF16)
        fix = dot(left, jnp.concatenate([there, there], axis=0))
        own = slice(0, 16) if j % 2 == 0 else slice(16, 32)
        for c in range(10):
            for t in range(2):
                lanes = slice(128 * t, 128 * t + 128)
                theirs = halo[j][0, c, :, lanes] + fix[16 * c : 16 * c + 16, lanes]
                if j < 2:
                    mine = xt[c, j, own, lanes]
                else:
                    y = j - 2
                    mine = yt[c, t, own, 128 * y : 128 * y + 128]
                hal[j, c, :, lanes] = jnp.where(present, theirs, mine)


def faces_xy(xt, yt, hal, hx, hy):
    for face in range(3):
        for t in range(2):
            lanes = slice(128 * t, 128 * t + 128)
            left = [hal[0, c, :, lanes] if face == 0 else xt[c, face - 1, 16:32, lanes] for c in range(10)]
            right = [hal[1, c, :, lanes] if face == 2 else xt[c, face, 0:16, lanes] for c in range(10)]
            out, _, _ = common(left, right, 0)
            for c in range(10):
                hx[c, face, :, lanes] = out[c]
    for face in range(3):
        for x in range(2):
            mine = slice(128 * x, 128 * x + 128)
            before = slice(128 * face - 128, 128 * face)
            after = slice(128 * face, 128 * face + 128)
            left = [hal[2, c, :, mine] if face == 0 else yt[c, x, 16:32, before] for c in range(10)]
            right = [hal[3, c, :, mine] if face == 2 else yt[c, x, 0:16, after] for c in range(10)]
            out, _, _ = common(left, right, 1)
            for c in range(10):
                h = out[c].astype(BF16)
                if face < 2:
                    hy[c, x, 0:16, after] = h
                if face > 0:
                    hy[c, x, 16:32, before] = h


def faces_z(zt, hz):
    edge = iota((16, 128), 1) == 0
    for t in range(2):
        lanes = slice(128 * t, 128 * t + 128)
        for x in range(2):
            left = [pltpu.roll(zt[c, x, 16:32, lanes], 1, 1) for c in range(10)]
            right = [zt[c, x, 0:16, lanes] for c in range(10)]
            out, fl, fr = common(left, right, 2)
            for c in range(10):
                hz[c, x, 0:16, lanes] = jnp.where(edge, fr[c], out[c]).astype(BF16)
                hz[c, x, 16:32, lanes] = pltpu.roll(jnp.where(edge, fl[c], out[c]), 127, 1).astype(BF16)


def point_fluxes(now, vol):
    @pl.loop(0, 8, unroll=2)
    def _(i):
        x, q = i // 4, pl.multiple_of((i % 4) * 16, 16)
        for t in range(2):
            lanes = slice(128 * t, 128 * t + 128)
            w = [now[c, x, pl.ds(q, 16), lanes] for c in range(10)]
            u, du = w[:5], w[5:]
            r, v, vv, p = primitive(u)
            dv, dp = tangent(du, r, v, vv)
            for d in range(3):
                f, df = flux(u, du, v, p, dv, dp, d)
                for c in range(10):
                    vol[c, x, pl.ds(64 * d + q, 16), lanes] = (f + df)[c].astype(BF16)


def lift_x(hx, c, x, a, scale):
    return float(-scale * LIFT_HI[a]) * hx[c, x + 1] + float(scale * LIFT_LO[a]) * hx[c, x]


def first_section_kernel(field, req, resp, trow, tcol, main_t, trace_t, *refs):
    halo, info, (now_ref, result, resp_out), scratch = refs[0:4], refs[4:8], refs[8:11], refs[11:]
    now, got, lhs, xt, yt, zt, hal, hx, hy, hz, vol, asked, picks = scratch
    g = pl.program_id(0)

    @pl.when(g == 0)
    def _():
        got[...] = resp[...].T
        load_asked(req, asked)

    set_fringe(field, got, trow, tcol, 0, g, lhs, now)
    all_traces(now, trace_t, xt, yt, zt)
    mend_halos(halo, info, got, 0, g, xt, yt, hal)
    faces_xy(xt, yt, hal, hx, hy)
    faces_z(zt, hz)
    point_fluxes(now, vol)
    for x in range(2):
        for c in range(10):
            res = dot(main_t[...], jnp.concatenate([vol[c, x], hz[c, x], hy[c, x]], axis=0))
            for a in range(4):
                rows = slice(16 * a, 16 * a + 16)
                mine = now[c, x, rows]
                now_ref[c // 5, c % 5, 0, x, rows] = mine
                result[c // 5, c % 5, 0, x, rows] = mine + (res[rows] + lift_x(hx, c, x, a, DT))
    for x in range(2):
        rows = jnp.concatenate([result[c // 5, c % 5, 0, x] for c in range(10)], axis=0)
        start = (g == 0) if x == 0 else jnp.bool_(False)
        interpolate_part(rows, asked, 1, g * 512 + x * 256, picks, start)

    @pl.when(g == 1)
    def _():
        resp_out[...] = answer(asked, 1, picks)


def inner_kernel(field, first, resp, trow, tcol, main_t, trace_t, partial_out, xt_out, yt_out, *scratch):
    now, got, lhs, zt, hz, vol = scratch
    g = pl.program_id(0)

    @pl.when(g == 0)
    def _():
        got[...] = resp[...].T

    set_fringe(field, got, trow, tcol, 1, g, lhs, now)
    all_traces(now, trace_t, xt_out.at[0], yt_out.at[0], zt)
    faces_z(zt, hz)
    point_fluxes(now, vol)
    for x in range(2):
        for c in range(10):
            res = dot(main_t[...], jnp.concatenate([vol[c, x], hz[c, x]], axis=0))
            partial_out[c // 5, c % 5, 0, x] = 0.5 * (now[c, x] + first[c // 5, c % 5, 0, x]) + res


def outer_kernel(part, xt, yt, resp, lift_y, *refs):
    halo, info, result, (got, hal, hx, hy) = refs[0:4], refs[4:8], refs[8], refs[9:]
    g = pl.program_id(0)

    @pl.when(g == 0)
    def _():
        got[...] = resp[...].T

    mend_halos(halo, info, got, 1, g, xt.at[0], yt.at[0], hal)
    faces_xy(xt.at[0], yt.at[0], hal, hx, hy)
    for x in range(2):
        for c in range(10):
            res = dot(lift_y[...], hy[c, x])
            for a in range(4):
                rows = slice(16 * a, 16 * a + 16)
                add = res[rows] + lift_x(hx, c, x, a, 0.5 * DT)
                result[c // 5, c % 5, 0, x, rows] = part[c // 5, c % 5, 0, x, rows] + add


FIELD = (2, 5, 2, 2, 64, 256)


def field_spec():
    return pl.BlockSpec((2, 5, 1, 2, 64, 256), lambda g: (0, 0, g, 0, 0, 0))


def whole(shape):
    return pl.BlockSpec(shape, lambda g: (0,) * len(shape))


def halo_spec(comps):
    return pl.BlockSpec((1, comps, 16, 256), lambda g: (g, 0, 0, 0))


def shape(*dims):
    return jax.ShapeDtypeStruct(dims, F32)


def params(mb):
    return pltpu.CompilerParams(dimension_semantics=("arbitrary",), vmem_limit_bytes=mb * 2**20)


def shift(x, axis, up):
    n = lax.axis_size(axis)
    pairs = [(i, i + 1) if up else (i + 1, i) for i in range(n - 1)]
    return lax.ppermute(x, axis, pairs)


def to_neighbours(traces):
    xlo, xhi, ylo, yhi = traces
    return [
        shift(xhi, "rotor", True),
        shift(xlo, "rotor", False),
        shift(yhi, "tower", True),
        shift(ylo, "tower", False),
    ]


def exchange(x):
    return lax.all_to_all(x, AXES, split_axis=0, concat_axis=0, tiled=True)


def estimate(us):
    return pl.CostEstimate(flops=int(us * 10**9), bytes_accessed=10**5, transcendentals=0)


def vmem(*dims, dtype=F32):
    return pltpu.VMEM(dims, dtype)


def far(x):
    return pltpu.with_memory_space_constraint(x, pltpu.HBM)


def info_specs():
    return [pl.BlockSpec((1, 1, 16, 256), lambda g: (0, 10, 0, 0))] * 4


def table(scale, columns):
    return jnp.asarray((scale * MAIN[:, columns]).astype(np.float32), BF16)


def trace_call(sec, field, trow, tcol):
    comps = 10 + (sec == 0)
    return pl.pallas_call(
        partial(trace_kernel, sec),
        grid=(2,),
        in_specs=[field_spec(), whole((8, 256)), whole((256, 128)), whole((96, 192))],
        out_specs=[halo_spec(comps)] * 4,
        out_shape=[shape(2, comps, 16, 256)] * 4,
        compiler_params=params(16),
        cost_estimate=estimate(2),
        name="traces",
    )(far(field), trow, tcol, jnp.asarray(TRACE))


def first_section(field, req, resp, trow, tcol, halos):
    return pl.pallas_call(
        first_section_kernel,
        grid=(2,),
        in_specs=[field_spec(), whole((384, 128)), whole((128, 128)), whole((8, 256)), whole((256, 128))]
        + [whole((64, 256)), whole((96, 192))]
        + [halo_spec(10)] * 4
        + info_specs(),
        out_specs=[field_spec(), field_spec(), whole((128, 128))],
        out_shape=[pltpu.HBM(FIELD, F32), pltpu.HBM(FIELD, F32), shape(128, 128)],
        scratch_shapes=[
            vmem(10, 2, 64, 256),
            vmem(128, 128),
            vmem(640, 512, dtype=BF16),
            vmem(10, 2, 32, 256),
            vmem(10, 2, 32, 256),
            vmem(10, 2, 32, 256),
            vmem(4, 10, 16, 256),
            vmem(10, 3, 16, 256),
            vmem(10, 2, 32, 256, dtype=BF16),
            vmem(10, 2, 32, 256, dtype=BF16),
            vmem(10, 2, 192, 256, dtype=BF16),
            vmem(384, 128),
            vmem(640, 256),
        ],
        compiler_params=params(28),
        cost_estimate=estimate(10),
        name="first_section",
    )(far(field), req, resp, trow, tcol, table(-DT, slice(0, 256)), jnp.asarray(TRACE), *halos, *halos)


def inner(field, first, resp, trow, tcol):
    side_spec = pl.BlockSpec((1, 10, 2, 32, 256), lambda g: (g, 0, 0, 0, 0))
    return pl.pallas_call(
        inner_kernel,
        grid=(2,),
        in_specs=[field_spec(), field_spec(), whole((128, 128)), whole((8, 256)), whole((256, 128))]
        + [whole((64, 224)), whole((96, 192))],
        out_specs=[field_spec(), side_spec, side_spec],
        out_shape=[shape(*FIELD), shape(2, 10, 2, 32, 256), shape(2, 10, 2, 32, 256)],
        scratch_shapes=[
            vmem(10, 2, 64, 256),
            vmem(128, 128),
            vmem(640, 512, dtype=BF16),
            vmem(10, 2, 32, 256),
            vmem(10, 2, 32, 256, dtype=BF16),
            vmem(10, 2, 192, 256, dtype=BF16),
        ],
        compiler_params=params(24),
        cost_estimate=estimate(100),
        name="inner",
    )(far(field), far(first), resp, trow, tcol, table(-0.5 * DT, slice(0, 224)), jnp.asarray(TRACE))


def outer(part, xt, yt, resp, halos, infos):
    side_spec = pl.BlockSpec((1, 10, 2, 32, 256), lambda g: (g, 0, 0, 0, 0))
    return pl.pallas_call(
        outer_kernel,
        grid=(2,),
        in_specs=[field_spec(), side_spec, side_spec, whole((128, 128)), whole((64, 32))]
        + [halo_spec(10)] * 4
        + info_specs(),
        out_specs=field_spec(),
        out_shape=shape(*FIELD),
        scratch_shapes=[
            vmem(128, 128),
            vmem(4, 10, 16, 256),
            vmem(10, 3, 16, 256),
            vmem(10, 2, 32, 256, dtype=BF16),
        ],
        compiler_params=params(24),
        cost_estimate=estimate(10),
        name="outer",
    )(part, xt, yt, resp, table(-0.5 * DT, slice(224, 256)), *halos, *infos)


def on_device(field, owner, donor, target, weight):
    req, trow, tcol = pl.pallas_call(
        request_kernel,
        out_shape=[shape(384, 128), shape(8, 256), shape(256, 128)],
        compiler_params=pltpu.CompilerParams(vmem_limit_bytes=16 * 2**20),
        name="request",
    )(
        far(owner.reshape(2, DEV)),
        far(donor.reshape(2, DEV)),
        far(target.reshape(2, DEV)),
        far(jnp.swapaxes(weight[0, 0], 1, 2)),
    )
    req = exchange(req)
    infos = to_neighbours(trace_call(0, field, trow, tcol))
    resp = pl.pallas_call(
        interpolate_kernel,
        grid=(4,),
        in_specs=[
            pl.BlockSpec((2, 5, 1, 1, 64, 256), lambda i: (0, 0, i // 2, i % 2, 0, 0)),
            whole((384, 128)),
        ],
        out_specs=whole((128, 128)),
        out_shape=shape(128, 128),
        scratch_shapes=[vmem(384, 128), vmem(640, 256)],
        compiler_params=params(16),
        cost_estimate=estimate(100),
        name="interpolate",
    )(far(field), req)
    resp = exchange(resp)
    first, middle, resp = first_section(field, req, resp, trow, tcol, infos)
    resp = exchange(resp)
    halos = to_neighbours(trace_call(1, middle, trow, tcol))
    part, xt, yt = inner(middle, first, resp, trow, tcol)
    return outer(part, xt, yt, resp, halos, infos)


def solution(mesh):
    placed = (
        P(None, None, None, "rotor", None, "tower"),
        P("rotor", "tower", None, None, None),
        P("rotor", "tower", None, None),
        P("rotor", "tower", None, None),
        P("rotor", "tower", None, None, None),
    )
    return jax.shard_map(
        on_device,
        mesh=mesh,
        in_specs=placed,
        out_specs=P(None, None, None, "rotor", None, "tower"),
        check_vma=False,
    )
```

time: 114 us -> 98.2 us (0.86)
  the two profiles are of different devices: /device:TPU:1 before, /device:TPU:14 now
where the time goes in v1:
time: 98.2 us; the launch traced here: 97.6 us
  starting transfers between devices  40.1 us (41%)
  Pallas kernels  33.3 us (34%)
  blocking collectives  17.2 us (18%)
  waiting for transfers between devices  4.14 us (4%)
  local copies, waits for them, and re-layouts  2.67 us (3%)
    ppermute x8, starting transfers between devices, shift(): return lax.ppermute(x, axis, pairs)  22.8 us
    all_to_all x2, starting transfers between devices, exchange(): return lax.all_to_all(x, AXES, split_axis=0, concat_axis=0, tiled=True)  17.3 us
    all_to_all x1, blocking collectives, exchange(): return lax.all_to_all(x, AXES, split_axis=0, concat_axis=0, tiled=True)  17.2 us
    pallas_call x1, Pallas kernels, first_section(): pl.pallas_call(first_section_kernel, grid=(2,), in_specs=[field_spec(), w...  11.1 us
    pallas_call x1, Pallas kernels, inner(): pl.pallas_call(inner_kernel, grid=(2,), in_specs=[field_spec(), field_spe...  6.75 us
    pallas_call x2, Pallas kernels, trace_call(): pl.pallas_call(partial(trace_kernel, sec), grid=(2,), in_specs=[field_spe...  6.11 us
    pallas_call x1, Pallas kernels, outer(): pl.pallas_call(outer_kernel, grid=(2,), in_specs=[field_spec(), side_spec...  4.2 us
    ppermute x8, waiting for transfers between devices, shift(): return lax.ppermute(x, axis, pairs)  4.14 us
  transfers between devices with their start and end apart: 10, of which 1 were waited for; matrix products, arithmetic and copies ran while one was open for 0% of the time, Pallas kernels for 17%

profile of v1, /device:TPU:14, one launch (start us, length us, event | category | flops | bytes accessed | tf_op | source)
XLA Modules:
  0.0 97.6 jit_solution(1247363347335721318)
XLA Ops:
  0.0 1.6 %request.1 = (f32[384,128]{1,0:T(8,128)S(1)}, f32[8,256]{1,0:T(8,128)S(1)}, f32[256,128]{1,0:T(8,128)S(1)}) custom-call(s32[2,128]{1,0:T(2,128)} %bitcast.19, s32[2,128]{1,0:T(2,128)} %bitcast.20, s32[2,128]{1,0:T(2,128)} %bitcast.21, f32[2,64,128]{2,1,0:T(8,128)} %bitcast.18), custom_call_target="tpu_custom_call" | custom-call | tf_op jit(solution)/shard_map/request/pallas_call | solution.py:626
  1.6 0.8 all_to_all.21
  2.4 10.8 %all-to-all-start = ((f32[128,3,128]{2,1,0:T(4,128)}), f32[128,3,128]{2,1,0:T(4,128)}, u32[]{:S(2)}, u32[]{:S(2)}) async-start(f32[128,3,128]{2,1,0:T(4,128)} %all_to_all.21), calls=%async_computation | async-start | bytes 524288 | tf_op jit(solution)/shard_map/all_to_all | solution.py:512
  13.2 0.0 copy-start
  13.2 0.8 copy-done
  14.0 2.7 %traces.2 = (f32[2,11,16,256]{3,2,1,0:T(8,128)S(1)}, f32[2,11,16,256]{3,2,1,0:T(8,128)S(1)}, f32[2,11,16,256]{3,2,1,0:T(8,128)S(1)}, f32[2,11,16,256]{3,2,1,0:T(8,128)S(1)}) custom-call(f32[2,5,2,2,64,256]{5,4,3,2,1,0:T(8,128)} %field.5, f32[8,256]{1,0:T(8,128)S(1)} %get-tuple-element.23.trow, f32[256,128]{1,0:T(8,128)S(1)} %get-tuple-element.24.tcol, ...), custom_call_target="tpu_custom_call" | custom-call | flops 2000000000 | bytes 100000 | tf_op jit(solution)/shard_map/traces/pallas_call | solution.py:537
  16.7 2.1 %collective-permute-start = (f32[2,11,16,256]{3,2,1,0:T(8,128)S(1)}, f32[2,11,16,256]{3,2,1,0:T(8,128)S(1)}, u32[]{:S(2)}, u32[]{:S(2)}) collective-permute-start(f32[2,11,16,256]{3,2,1,0:T(8,128)S(1)} %get-tuple-element.25), channel_id=1, source_target_pairs={{0,16},{16,32},{32,48},{48,64},{64,80},{80,96},{96,112},{1,17},{17... | collective-permute-start | bytes 1081352 | tf_op jit(solution)/shard_map/ppermute | solution.py:498
  18.8 3.5 %collective-permute-start.1 = (f32[2,11,16,256]{3,2,1,0:T(8,128)S(1)}, f32[2,11,16,256]{3,2,1,0:T(8,128)S(1)}, u32[]{:S(2)}, u32[]{:S(2)}) collective-permute-start(f32[2,11,16,256]{3,2,1,0:T(8,128)S(1)} %get-tuple-element.26), channel_id=1, source_target_pairs={{16,0},{32,16},{48,32},{64,48},{80,64},{96,80},{112,96},{17,1},{33... | collective-permute-start | bytes 1081352 | tf_op jit(solution)/shard_map/ppermute | solution.py:498
  22.3 3.6 %collective-permute-start.2 = (f32[2,11,16,256]{3,2,1,0:T(8,128)S(1)}, f32[2,11,16,256]{3,2,1,0:T(8,128)S(1)}, u32[]{:S(2)}, u32[]{:S(2)}) collective-permute-start(f32[2,11,16,256]{3,2,1,0:T(8,128)S(1)} %get-tuple-element.27), channel_id=1, source_target_pairs={{0,1},{1,2},{2,3},{3,4},{4,5},{5,6},{6,7},{7,8},{8,9},{9,10},{10,1... | collective-permute-start | bytes 1081352 | tf_op jit(solution)/shard_map/ppermute | solution.py:498
  25.8 2.3 %collective-permute-start.3 = (f32[2,11,16,256]{3,2,1,0:T(8,128)S(1)}, f32[2,11,16,256]{3,2,1,0:T(8,128)S(1)}, u32[]{:S(2)}, u32[]{:S(2)}) collective-permute-start(f32[2,11,16,256]{3,2,1,0:T(8,128)S(1)} %get-tuple-element.28), channel_id=1, source_target_pairs={{1,0},{2,1},{3,2},{4,3},{5,4},{6,5},{7,6},{8,7},{9,8},{10,9},{11,1... | collective-permute-start | bytes 1081352 | tf_op jit(solution)/shard_map/ppermute | solution.py:498
  28.1 0.0 all-to-all-done
  28.2 1.0 %all_to_all.23.req = f32[384,128]{1,0:T(8,128)S(1)} reshape(f32[128,3,128]{2,1,0:T(4,128)} %all-to-all-done) | data formatting | bytes 393216 | tf_op jit(solution)/shard_map/all_to_all | solution.py:512
  29.2 0.0 copy-start.3
  29.2 3.6 %interpolate.1 = f32[128,128]{1,0:T(8,128)S(1)} custom-call(f32[2,5,2,2,64,256]{5,4,3,2,1,0:T(8,128)} %field.5, f32[384,128]{1,0:T(8,128)S(1)} %all_to_all.23.req), custom_call_target="tpu_custom_call" | custom-call | flops 99999997952 | bytes 100000 | tf_op jit(solution)/shard_map/interpolate/pallas_call | solution.py:639
  32.8 17.2 %all_to_all.33 = f32[128,1,128]{2,1,0:T(1,128)S(1)} all-to-all(f32[128,1,128]{2,1,0:T(1,128)S(1)} %bitcast.17), channel_id=1, replica_groups=mesh['rotor'=8,'tower'=16] {'rotor','tower'}, dimensions={0} | all-to-all | bytes 131072 | tf_op jit(solution)/shard_map/all_to_all | solution.py:512
  50.0 0.0 collective-permute-done.refs_0_.refs_4_
  50.0 0.0 collective-permute-done.1.refs_1_.refs_5_
  50.0 0.0 collective-permute-done.2.refs_2_.refs_6_
  50.0 0.0 collective-permute-done.3.refs_3_.refs_7_
  50.0 0.0 copy-done.3
  50.0 11.1 %first_section.1 = (f32[2,5,2,2,64,256]{5,4,3,2,1,0:T(8,128)}, f32[2,5,2,2,64,256]{5,4,3,2,1,0:T(8,128)}, f32[128,128]{1,0:T(8,128)}) custom-call(f32[2,5,2,2,64,256]{5,4,3,2,1,0:T(8,128)} %field.5, f32[384,128]{1,0:T(8,128)S(1)} %all_to_all.23.req, f32[128,128]{1,0:T(8,128)S(1)} %bitcast.16, f32[8,256]{1,0:T(8,128)S(1)} %get-tuple-element.23.trow, ...), custom_call_target="tpu_custom_call" | custom-call | flops 10000000000 | bytes 100000 | tf_op jit(solution)/shard_map/first_section/pallas_call | solution.py:550
  61.1 6.5 %all-to-all-start.2 = ((f32[128,1,128]{2,1,0:T(1,128)}), f32[128,1,128]{2,1,0:T(1,128)S(1)}, u32[]{:S(2)}, u32[]{:S(2)}) async-start(f32[128,1,128]{2,1,0:T(1,128)} %bitcast.9), calls=%async_computation.2 | async-start | bytes 131072 | tf_op jit(solution)/shard_map/all_to_all | solution.py:512
  67.6 0.0 copy-start.1
  67.6 0.0 copy-start.2
  67.6 3.4 %traces.3 = (f32[2,10,16,256]{3,2,1,0:T(8,128)}, f32[2,10,16,256]{3,2,1,0:T(8,128)}, f32[2,10,16,256]{3,2,1,0:T(8,128)S(1)}, f32[2,10,16,256]{3,2,1,0:T(8,128)}) custom-call(f32[2,5,2,2,64,256]{5,4,3,2,1,0:T(8,128)} %get-tuple-element.29.field, f32[8,256]{1,0:T(8,128)S(1)} %get-tuple-element.23.trow, f32[256,128]{1,0:T(8,128)S(1)} %get-tuple-element.24.tcol, ...), custom_call_target="tpu_custom_call" | custom-call | flops 2000000000 | bytes 100000 | tf_op jit(solution)/shard_map/traces/pallas_call | solution.py:537
  71.0 2.0 %collective-permute-start.4 = (f32[2,10,16,256]{3,2,1,0:T(8,128)}, f32[2,10,16,256]{3,2,1,0:T(8,128)S(1)}, u32[]{:S(2)}, u32[]{:S(2)}) collective-permute-start(f32[2,10,16,256]{3,2,1,0:T(8,128)} %get-tuple-element.35), channel_id=1, source_target_pairs={{0,16},{16,32},{32,48},{48,64},{64,80},{80,96},{96,112},{1,17},{17... | collective-permute-start | bytes 983048 | tf_op jit(solution)/shard_map/ppermute | solution.py:498
  73.1 3.5 %collective-permute-start.5 = (f32[2,10,16,256]{3,2,1,0:T(8,128)}, f32[2,10,16,256]{3,2,1,0:T(8,128)S(1)}, u32[]{:S(2)}, u32[]{:S(2)}) collective-permute-start(f32[2,10,16,256]{3,2,1,0:T(8,128)} %get-tuple-element.36), channel_id=1, source_target_pairs={{16,0},{32,16},{48,32},{64,48},{80,64},{96,80},{112,96},{17,1},{33... | collective-permute-start | bytes 983048 | tf_op jit(solution)/shard_map/ppermute | solution.py:498
  76.6 3.6 %collective-permute-start.6 = (f32[2,10,16,256]{3,2,1,0:T(8,128)}, f32[2,10,16,256]{3,2,1,0:T(8,128)S(1)}, u32[]{:S(2)}, u32[]{:S(2)}) collective-permute-start(f32[2,10,16,256]{3,2,1,0:T(8,128)} %get-tuple-element.37), channel_id=1, source_target_pairs={{0,1},{1,2},{2,3},{3,4},{4,5},{5,6},{6,7},{7,8},{8,9},{9,10},{10,1... | collective-permute-start | bytes 983048 | tf_op jit(solution)/shard_map/ppermute | solution.py:498
  80.1 2.3 %collective-permute-start.7 = (f32[2,10,16,256]{3,2,1,0:T(8,128)S(1)}, f32[2,10,16,256]{3,2,1,0:T(8,128)S(1)}, u32[]{:S(2)}, u32[]{:S(2)}) collective-permute-start(f32[2,10,16,256]{3,2,1,0:T(8,128)S(1)} %get-tuple-element.38), channel_id=1, source_target_pairs={{1,0},{2,1},{3,2},{4,3},{5,4},{6,5},{7,6},{8,7},{9,8},{10,9},{11,1... | collective-permute-start | bytes 983048 | tf_op jit(solution)/shard_map/ppermute | solution.py:498
  82.4 0.0 all-to-all-done.2
  82.4 0.0 copy-done.1
  82.5 0.0 copy-done.2
  82.5 0.0 copy-start.4
  82.5 6.8 %inner.1 = (f32[2,5,2,2,64,256]{5,4,3,2,1,0:T(8,128)S(1)}, f32[2,10,2,32,256]{4,3,2,1,0:T(8,128)S(1)}, f32[2,10,2,32,256]{4,3,2,1,0:T(8,128)S(1)}) custom-call(f32[2,5,2,2,64,256]{5,4,3,2,1,0:T(8,128)} %get-tuple-element.29.field, f32[2,5,2,2,64,256]{5,4,3,2,1,0:T(8,128)} %get-tuple-element.30.first, f32[128,128]{1,0:T(8,128)S(1)} %bitcast.14, ...), custom_call_target="tpu_custom_call" | custom-call | flops 99999997952 | bytes 100000 | tf_op jit(solution)/shard_map/inner/pallas_call | solution.py:582
  89.2 0.0 collective-permute-done.4.refs_0_
  89.2 0.0 collective-permute-done.5.refs_1_
  89.3 0.0 collective-permute-done.6.refs_2_
  89.3 4.1 %collective-permute-done.7.refs_3_ = f32[2,10,16,256]{3,2,1,0:T(8,128)S(1)} collective-permute-done((f32[2,10,16,256]{3,2,1,0:T(8,128)S(1)}, f32[2,10,16,256]{3,2,1,0:T(8,128)S(1)}, u32[]{:S(2)}, u32[]{:S(2)}) %collective-permute-start.7) | collective-permute-done | bytes 327712 | tf_op jit(solution)/shard_map/ppermute | solution.py:498
  93.4 0.0 copy-done.4
  93.4 4.2 %outer.1 = f32[2,5,2,2,64,256]{5,4,3,2,1,0:T(8,128)} custom-call(f32[2,5,2,2,64,256]{5,4,3,2,1,0:T(8,128)S(1)} %get-tuple-element.32.part, f32[2,10,2,32,256]{4,3,2,1,0:T(8,128)S(1)} %get-tuple-element.33.xt, f32[2,10,2,32,256]{4,3,2,1,0:T(8,128)S(1)} %get-tuple-element.34.yt, f32[128,128]{1,0:T(8,128)S(1)} %bitcast.15, bf16[64,32]{1,0:T(8,128)(2,1)S(1)} %copy-done.4, ...), custom_call_target="tpu_custom_call" | custom-call | flops 10000000000 | bytes 100000 | tf_op jit(solution)/shard_map/outer/pallas_call | solution.py:605
Async XLA Ops:
  2.4 25.8 %all-to-all-start = ((f32[128,3,128]{2,1,0:T(4,128)}), f32[128,3,128]{2,1,0:T(4,128)}, u32[]{:S(2)}, u32[]{:S(2)}) async-start(f32[128,3,128]{2,1,0:T(4,128)} %all_to_all.21), calls=%async_computation | async-start | bytes 524288 | tf_op jit(solution)/shard_map/all_to_all | solution.py:512
  13.2 0.8 copy-start
  16.7 33.3 %collective-permute-start = (f32[2,11,16,256]{3,2,1,0:T(8,128)S(1)}, f32[2,11,16,256]{3,2,1,0:T(8,128)S(1)}, u32[]{:S(2)}, u32[]{:S(2)}) collective-permute-start(f32[2,11,16,256]{3,2,1,0:T(8,128)S(1)} %get-tuple-element.25), channel_id=1, source_target_pairs={{0,16},{16,32},{32,48},{48,64},{64,80},{80,96},{96,112},{1,17},{17... | collective-permute-start | bytes 1081352 | tf_op jit(solution)/shard_map/ppermute | solution.py:498
  18.8 31.2 %collective-permute-start.1 = (f32[2,11,16,256]{3,2,1,0:T(8,128)S(1)}, f32[2,11,16,256]{3,2,1,0:T(8,128)S(1)}, u32[]{:S(2)}, u32[]{:S(2)}) collective-permute-start(f32[2,11,16,256]{3,2,1,0:T(8,128)S(1)} %get-tuple-element.26), channel_id=1, source_target_pairs={{16,0},{32,16},{48,32},{64,48},{80,64},{96,80},{112,96},{17,1},{33... | collective-permute-start | bytes 1081352 | tf_op jit(solution)/shard_map/ppermute | solution.py:498
  22.3 27.7 %collective-permute-start.2 = (f32[2,11,16,256]{3,2,1,0:T(8,128)S(1)}, f32[2,11,16,256]{3,2,1,0:T(8,128)S(1)}, u32[]{:S(2)}, u32[]{:S(2)}) collective-permute-start(f32[2,11,16,256]{3,2,1,0:T(8,128)S(1)} %get-tuple-element.27), channel_id=1, source_target_pairs={{0,1},{1,2},{2,3},{3,4},{4,5},{5,6},{6,7},{7,8},{8,9},{9,10},{10,1... | collective-permute-start | bytes 1081352 | tf_op jit(solution)/shard_map/ppermute | solution.py:498
  25.8 24.2 %collective-permute-start.3 = (f32[2,11,16,256]{3,2,1,0:T(8,128)S(1)}, f32[2,11,16,256]{3,2,1,0:T(8,128)S(1)}, u32[]{:S(2)}, u32[]{:S(2)}) collective-permute-start(f32[2,11,16,256]{3,2,1,0:T(8,128)S(1)} %get-tuple-element.28), channel_id=1, source_target_pairs={{1,0},{2,1},{3,2},{4,3},{5,4},{6,5},{7,6},{8,7},{9,8},{10,9},{11,1... | collective-permute-start | bytes 1081352 | tf_op jit(solution)/shard_map/ppermute | solution.py:498
  29.2 20.8 %copy-start.3 = (bf16[64,256]{1,0:T(8,128)(2,1)S(1)}, bf16[64,256]{1,0:T(8,128)(2,1)}, u32[]{:S(2)}) copy-start(bf16[64,256]{1,0:T(8,128)(2,1)} %constant.9.clone.main_t) | copy-start | bytes 98308
  61.1 21.3 %all-to-all-start.2 = ((f32[128,1,128]{2,1,0:T(1,128)}), f32[128,1,128]{2,1,0:T(1,128)S(1)}, u32[]{:S(2)}, u32[]{:S(2)}) async-start(f32[128,1,128]{2,1,0:T(1,128)} %bitcast.9), calls=%async_computation.2 | async-start | bytes 131072 | tf_op jit(solution)/shard_map/all_to_all | solution.py:512
  67.6 14.9 %copy-start.1 = (bf16[96,192]{1,0:T(8,128)(2,1)S(1)}, bf16[96,192]{1,0:T(8,128)(2,1)}, u32[]{:S(2)}) copy-start(bf16[96,192]{1,0:T(8,128)(2,1)} %constant.8.clone.table.trace_t) | copy-start | bytes 110596
  67.6 14.9 %copy-start.2 = (bf16[64,224]{1,0:T(8,128)(2,1)S(1)}, bf16[64,224]{1,0:T(8,128)(2,1)}, u32[]{:S(2)}) copy-start(bf16[64,224]{1,0:T(8,128)(2,1)} %constant.10.clone.main_t) | copy-start | bytes 86020
  71.0 18.2 %collective-permute-start.4 = (f32[2,10,16,256]{3,2,1,0:T(8,128)}, f32[2,10,16,256]{3,2,1,0:T(8,128)S(1)}, u32[]{:S(2)}, u32[]{:S(2)}) collective-permute-start(f32[2,10,16,256]{3,2,1,0:T(8,128)} %get-tuple-element.35), channel_id=1, source_target_pairs={{0,16},{16,32},{32,48},{48,64},{64,80},{80,96},{96,112},{1,17},{17... | collective-permute-start | bytes 983048 | tf_op jit(solution)/shard_map/ppermute | solution.py:498
  73.1 16.2 %collective-permute-start.5 = (f32[2,10,16,256]{3,2,1,0:T(8,128)}, f32[2,10,16,256]{3,2,1,0:T(8,128)S(1)}, u32[]{:S(2)}, u32[]{:S(2)}) collective-permute-start(f32[2,10,16,256]{3,2,1,0:T(8,128)} %get-tuple-element.36), channel_id=1, source_target_pairs={{16,0},{32,16},{48,32},{64,48},{80,64},{96,80},{112,96},{17,1},{33... | collective-permute-start | bytes 983048 | tf_op jit(solution)/shard_map/ppermute | solution.py:498
  76.6 12.7 %collective-permute-start.6 = (f32[2,10,16,256]{3,2,1,0:T(8,128)}, f32[2,10,16,256]{3,2,1,0:T(8,128)S(1)}, u32[]{:S(2)}, u32[]{:S(2)}) collective-permute-start(f32[2,10,16,256]{3,2,1,0:T(8,128)} %get-tuple-element.37), channel_id=1, source_target_pairs={{0,1},{1,2},{2,3},{3,4},{4,5},{5,6},{6,7},{7,8},{8,9},{9,10},{10,1... | collective-permute-start | bytes 983048 | tf_op jit(solution)/shard_map/ppermute | solution.py:498
  80.1 13.2 %collective-permute-start.7 = (f32[2,10,16,256]{3,2,1,0:T(8,128)S(1)}, f32[2,10,16,256]{3,2,1,0:T(8,128)S(1)}, u32[]{:S(2)}, u32[]{:S(2)}) collective-permute-start(f32[2,10,16,256]{3,2,1,0:T(8,128)S(1)} %get-tuple-element.38), channel_id=1, source_target_pairs={{1,0},{2,1},{3,2},{4,3},{5,4},{6,5},{7,6},{8,7},{9,8},{10,9},{11,1... | collective-permute-start | bytes 983048 | tf_op jit(solution)/shard_map/ppermute | solution.py:498
  82.5 10.9 %copy-start.4 = (bf16[64,32]{1,0:T(8,128)(2,1)S(1)}, bf16[64,32]{1,0:T(8,128)(2,1)}, u32[]{:S(2)}) copy-start(bf16[64,32]{1,0:T(8,128)(2,1)} %constant.11.clone.lift_y) | copy-start | bytes 12292

commit v2 on v1

--- a/solution.py
+++ b/solution.py
@@ -167,16 +167,26 @@
             tc[s] = jnp.where(lane == sec, res[:, 65:66], tc[s])
     for sec in range(2):
         pair = jnp.where(lane < 64, results[2 * sec], pltpu.roll(results[2 * sec + 1], 64, 1))
-        req[pl.ds(sec, DEV, stride=3), :] = pair
+        req[pl.ds(sec, DEV, stride=4), :] = pair
     ids = jnp.zeros((DEV, DEV), F32)
     for i in range(4):
         ids = jnp.where(lane == i, results[i][:, 64:65], ids)
-    req[pl.ds(2, DEV, stride=3), :] = ids
+    req[pl.ds(2, DEV, stride=4), :] = ids
+    req[pl.ds(3, DEV, stride=4), :] = jnp.zeros((DEV, DEV), F32)
     for s in range(2):
         tcol[s * 128 : s * 128 + 128, :] = tc[s]
         trow[:, s * 128 : s * 128 + 128] = tc[s].T[0:8]
 
 
+def block_in(field, buf, sem, i):
+    return pltpu.make_async_copy(field.at[:, :, i // 2, i % 2], buf.at[i], sem.at[i])
+
+
+def start_field(field, buf, sem):
+    for i in range(4):
+        block_in(field, buf, sem, i).start()
+
+
 def point_row(trow, sec):
     return (trow[sec : sec + 1, :].astype(I32) - 1) >> 9
 
@@ -185,56 +195,47 @@
     return jnp.broadcast_to((tcol[:, sec : sec + 1].astype(I32) - 1) & 511, (256, count))
 
 
-def target_mask(trow, tcol, sec, g):
-    at = jnp.where(iota((64, 256), 0) + 64 * g == point_row(trow, sec), 1.0, 0.0).astype(BF16)
-    where = jnp.where(iota((256, 512), 1) == element_col(tcol, sec, 512), 1.0, 0.0).astype(BF16)
-    return dot(at, where)
-
-
-def outer_traces(get, mask, trace_table, outs):
-    xlo, xhi, ylo, yhi = outs
-    keep = [mask[:, x * 256 : x * 256 + 256] < 0.5 for x in range(2)]
-    e2 = trace_table[32:64, :]
-    for c in range(10):
-        w = [jnp.where(keep[x], get(c, x), 0.0) for x in range(2)]
-        xlo[0, c] = sum(float(LOW[a]) * w[0][16 * a : 16 * a + 16] for a in range(4))
-        xhi[0, c] = sum(float(HIGHV[a]) * w[1][16 * a : 16 * a + 16] for a in range(4))
-        for y, out in ((0, ylo), (1, yhi)):
-            both = jnp.concatenate([w[x][:, y * 128 : y * 128 + 128] for x in range(2)], axis=1)
-            hi, lo = split(both)
-            res = dot(e2[16 * y : 16 * y + 16], jnp.concatenate([hi, lo, hi], axis=0))
-            out[0, c] = res
-
-
-def trace_kernel(sec, field, trow, tcol, table, *outs):
-    g = pl.program_id(0)
-    mask = target_mask(trow, tcol, sec, g)
-    outer_traces(lambda c, x: field[c // 5, c % 5, 0, x], mask, table, outs)
-    if sec == 1:
-        return
-    info = jnp.concatenate([trow[0:2, :], jnp.ones((1, 256), F32), jnp.zeros((13, 256), F32)], axis=0)
-    for out in outs:
-        out[0, 10] = info
+def trace_kernel(sec, field, trow, tcol, xlo, xhi, ylo, yhi, buf, sem):
+    start_field(field, buf, sem)
+    upper = iota((8, 128), 0) < 4
+    sides = [[jnp.where(upper, float(v[2 * k]), float(v[2 * k + 1])) for k in range(2)] for v in (LOW, HIGHV)]
+    if sec == 0:
+        info = jnp.concatenate([trow[0:2, :], jnp.ones((1, 256), F32), jnp.zeros((13, 256), F32)], axis=0)
+        for out in (xlo, xhi, ylo, yhi):
+            out[0, 10] = info
+            out[1, 10] = jnp.zeros((16, 256), F32)
+    for x in range(2):
+        there = iota((256, 256), 1) + 256 * x == element_col(tcol, sec, 256)
+        there = jnp.where(there, 1.0, 0.0).astype(BF16)
+        for g in range(2):
+            at = jnp.where(iota((64, 256), 0) + 64 * g == point_row(trow, sec), 1.0, 0.0).astype(BF16)
+            keep = dot(at, there) < 0.5
+            i = 2 * g + x
+            block_in(field, buf, sem, i).wait()
+            along, xout = ((LOW, xlo), (HIGHV, xhi))[x]
+            lanes = slice(128 * x, 128 * x + 128)
+            for c in range(10):
+                w = jnp.where(keep, buf[i, c // 5, c % 5], 0.0)
+                xout[g, c] = sum(float(along[a]) * w[16 * a : 16 * a + 16] for a in range(4))
+                for y, out in ((0, ylo), (1, yhi)):
+                    half = w[:, 128 * y : 128 * y + 128]
+                    rows = []
+                    for a in range(4):
+                        t = sides[y][0] * half[16 * a : 16 * a + 8] + sides[y][1] * half[16 * a + 8 : 16 * a + 16]
+                        rows.append(t + pltpu.roll(t, 4, 0))
+                    for k in range(2):
+                        out[g, c, 8 * k : 8 * k + 8, lanes] = jnp.where(upper, rows[2 * k], rows[2 * k + 1])
 
 
 def load_asked(req, asked):
     for i in range(3):
-        asked[i * 128 : i * 128 + 128, :] = req[pl.ds(i, DEV, stride=3), :].T
-
-
-def interpolate_part(field_rows, asked, sec, base, picks, first):
+        asked[i * 128 : i * 128 + 128, :] = req[pl.ds(i, DEV, stride=4), :].T
+
+
+def pick(asked, sec, donors):
     ids = asked[256 + 2 * sec : 256 + 2 * sec + 2, :]
     row = jnp.concatenate([ids[0:1], ids[1:2]], axis=1).astype(I32)
-    chosen = jnp.where(iota((256, 256), 0) + base == row, 1.0, 0.0).astype(BF16)
-    part = dot(field_rows.astype(BF16), chosen)
-
-    @pl.when(first)
-    def _():
-        picks[...] = part
-
-    @pl.when(jnp.logical_not(first))
-    def _():
-        picks[...] += part
+    return dot(donors[...], jnp.where(iota((1024, 256), 0) == row, 1.0, 0.0).astype(BF16))
 
 
 def answer(asked, sec, picks):
@@ -251,19 +252,15 @@
     return jnp.concatenate(groups, axis=0).T
 
 
-def interpolate_kernel(field, req, resp, asked, picks):
-    i = pl.program_id(0)
-
-    @pl.when(i == 0)
-    def _():
-        load_asked(req, asked)
-
-    rows = jnp.concatenate([field[c // 5, c % 5, 0, 0] for c in range(10)], axis=0)
-    interpolate_part(rows, asked, 0, i * 256, picks, i == 0)
-
-    @pl.when(i == 3)
-    def _():
-        resp[...] = answer(asked, 0, picks)
+def interpolate_kernel(field, req, resp, asked, picks, donors, buf, sem):
+    start_field(field, buf, sem)
+    load_asked(req, asked)
+    for i in range(4):
+        block_in(field, buf, sem, i).wait()
+        for c in range(10):
+            donors[64 * c : 64 * c + 64, 256 * i : 256 * i + 256] = buf[i, c // 5, c % 5].astype(BF16)
+    picks[...] = pick(asked, 0, donors)
+    resp[...] = answer(asked, 0, picks)
 
 
 def values(got, j):
@@ -271,7 +268,7 @@
     return jnp.concatenate([both[0:10], both[12:22]], axis=1)
 
 
-def set_fringe(field, got, trow, tcol, sec, g, lhs, now):
+def set_fringe(field, buf, sem, got, trow, tcol, sec, g, lhs, now):
     val = values(got, 0)
     at = iota((64, 256), 0) + 64 * g == point_row(trow, sec)
     for c in range(10):
@@ -283,9 +280,10 @@
     for x in range(2):
         wx = where[:, x * 256 : x * 256 + 256]
         scat = dot(lhs[...], jnp.concatenate([wx, wx], axis=0))
+        block_in(field, buf, sem, 2 * g + x).wait()
         hit = mask[:, x * 256 : x * 256 + 256] > 0.5
         for c in range(10):
-            now[c, x] = jnp.where(hit, scat[64 * c : 64 * c + 64], field[c // 5, c % 5, 0, x])
+            now[c, x] = jnp.where(hit, scat[64 * c : 64 * c + 64], buf[2 * g + x, c // 5, c % 5])
 
 
 def all_traces(now, table, xt, yt, zt):
@@ -300,8 +298,9 @@
 
 def mend_halos(halo, info, got, sec, g, xt, yt, hal):
     for j in range(4):
-        row2 = info[j][0, 0, sec : sec + 1, :]
-        present = info[j][0, 0, 2:3, 0:128] > 0.5
+        k = (j + 2) % 4
+        row2 = info[k][0, 10, sec : sec + 1, :]
+        present = info[k][0, 10, 2:3, 0:128] > 0.5
         pt = (row2.astype(I32) - 1) >> 9
         q = pt & 63
         elem = (row2.astype(I32) - 1) & 511
@@ -331,7 +330,7 @@
         for c in range(10):
             for t in range(2):
                 lanes = slice(128 * t, 128 * t + 128)
-                theirs = halo[j][0, c, :, lanes] + fix[16 * c : 16 * c + 16, lanes]
+                theirs = halo[k][g, c, :, lanes] + fix[16 * c : 16 * c + 16, lanes]
                 if j < 2:
                     mine = xt[c, j, own, lanes]
                 else:
@@ -398,59 +397,75 @@
     return float(-scale * LIFT_HI[a]) * hx[c, x + 1] + float(scale * LIFT_LO[a]) * hx[c, x]
 
 
+def blocks_out(src, dst, sem, g, x):
+    return [
+        pltpu.make_async_copy(src.at[g, pl.ds(5 * f, 5), x], dst.at[f, :, g, x], sem.at[g, x, f]) for f in range(2)
+    ]
+
+
 def first_section_kernel(field, req, resp, trow, tcol, main_t, trace_t, *refs):
-    halo, info, (now_ref, result, resp_out), scratch = refs[0:4], refs[4:8], refs[8:11], refs[11:]
-    now, got, lhs, xt, yt, zt, hal, hx, hy, hz, vol, asked, picks = scratch
+    halo, info, (now_out, mid_out, resp_out), scratch = refs[0:4], refs[4:8], refs[8:11], refs[11:]
+    nows, mids, got, lhs, xt, yt, zt, hal, hx, hy, hz, vol, asked, picks, donors, buf, sem, nsem, msem = scratch
     g = pl.program_id(0)
+    now, mid = nows.at[g], mids.at[g]
 
     @pl.when(g == 0)
     def _():
+        start_field(field, buf, sem)
         got[...] = resp[...].T
         load_asked(req, asked)
 
-    set_fringe(field, got, trow, tcol, 0, g, lhs, now)
+    set_fringe(field, buf, sem, got, trow, tcol, 0, g, lhs, now)
+    for x in range(2):
+        for copy in blocks_out(nows, now_out, nsem, g, x):
+            copy.start()
     all_traces(now, trace_t, xt, yt, zt)
     mend_halos(halo, info, got, 0, g, xt, yt, hal)
     faces_xy(xt, yt, hal, hx, hy)
     faces_z(zt, hz)
     point_fluxes(now, vol)
     for x in range(2):
+        columns = pl.ds(pl.multiple_of(512 * g + 256 * x, 256), 256)
         for c in range(10):
             res = dot(main_t[...], jnp.concatenate([vol[c, x], hz[c, x], hy[c, x]], axis=0))
             for a in range(4):
                 rows = slice(16 * a, 16 * a + 16)
-                mine = now[c, x, rows]
-                now_ref[c // 5, c % 5, 0, x, rows] = mine
-                result[c // 5, c % 5, 0, x, rows] = mine + (res[rows] + lift_x(hx, c, x, a, DT))
-    for x in range(2):
-        rows = jnp.concatenate([result[c // 5, c % 5, 0, x] for c in range(10)], axis=0)
-        start = (g == 0) if x == 0 else jnp.bool_(False)
-        interpolate_part(rows, asked, 1, g * 512 + x * 256, picks, start)
+                new = now[c, x, rows] + (res[rows] + lift_x(hx, c, x, a, DT))
+                mid[c, x, rows] = new
+                donors[64 * c + 16 * a : 64 * c + 16 * a + 16, columns] = new.astype(BF16)
+        for copy in blocks_out(mids, mid_out, msem, g, x):
+            copy.start()
 
     @pl.when(g == 1)
     def _():
+        picks[...] = pick(asked, 1, donors)
         resp_out[...] = answer(asked, 1, picks)
-
-
-def inner_kernel(field, first, resp, trow, tcol, main_t, trace_t, partial_out, xt_out, yt_out, *scratch):
-    now, got, lhs, zt, hz, vol = scratch
+        for h in range(2):
+            for x in range(2):
+                for copy in blocks_out(nows, now_out, nsem, h, x) + blocks_out(mids, mid_out, msem, h, x):
+                    copy.wait()
+
+
+def inner_kernel(field, resp, trow, tcol, main_t, trace_t, partial_out, xt_out, yt_out, *scratch):
+    now, got, lhs, zt, hz, vol, buf, sem = scratch
     g = pl.program_id(0)
 
     @pl.when(g == 0)
     def _():
+        start_field(field, buf, sem)
         got[...] = resp[...].T
 
-    set_fringe(field, got, trow, tcol, 1, g, lhs, now)
-    all_traces(now, trace_t, xt_out.at[0], yt_out.at[0], zt)
+    set_fringe(field, buf, sem, got, trow, tcol, 1, g, lhs, now)
+    all_traces(now, trace_t, xt_out.at[g], yt_out.at[g], zt)
     faces_z(zt, hz)
     point_fluxes(now, vol)
     for x in range(2):
         for c in range(10):
             res = dot(main_t[...], jnp.concatenate([vol[c, x], hz[c, x]], axis=0))
-            partial_out[c // 5, c % 5, 0, x] = 0.5 * (now[c, x] + first[c // 5, c % 5, 0, x]) + res
-
-
-def outer_kernel(part, xt, yt, resp, lift_y, *refs):
+            partial_out[c // 5, c % 5, g, x] = 0.5 * now[c, x] + res
+
+
+def outer_kernel(part, first, xt, yt, resp, lift_y, *refs):
     halo, info, result, (got, hal, hx, hy) = refs[0:4], refs[4:8], refs[8], refs[9:]
     g = pl.program_id(0)
 
@@ -458,15 +473,16 @@
     def _():
         got[...] = resp[...].T
 
-    mend_halos(halo, info, got, 1, g, xt.at[0], yt.at[0], hal)
-    faces_xy(xt.at[0], yt.at[0], hal, hx, hy)
+    mend_halos(halo, info, got, 1, g, xt.at[g], yt.at[g], hal)
+    faces_xy(xt.at[g], yt.at[g], hal, hx, hy)
     for x in range(2):
         for c in range(10):
             res = dot(lift_y[...], hy[c, x])
             for a in range(4):
                 rows = slice(16 * a, 16 * a + 16)
                 add = res[rows] + lift_x(hx, c, x, a, 0.5 * DT)
-                result[c // 5, c % 5, 0, x, rows] = part[c // 5, c % 5, 0, x, rows] + add
+                base = part[c // 5, c % 5, g, x, rows] + 0.5 * first[c // 5, c % 5, g, x, rows]
+                result[c // 5, c % 5, 0, x, rows] = base + add
 
 
 FIELD = (2, 5, 2, 2, 64, 256)
@@ -476,12 +492,12 @@
     return pl.BlockSpec((2, 5, 1, 2, 64, 256), lambda g: (0, 0, g, 0, 0, 0))
 
 
-def whole(shape):
-    return pl.BlockSpec(shape, lambda g: (0,) * len(shape))
-
-
-def halo_spec(comps):
-    return pl.BlockSpec((1, comps, 16, 256), lambda g: (g, 0, 0, 0))
+HERE = pl.BlockSpec(memory_space=pltpu.VMEM)
+AWAY = pl.BlockSpec(memory_space=pl.ANY)
+
+
+def blocks():
+    return [pltpu.VMEM((4, 2, 5, 64, 256), F32), pltpu.SemaphoreType.DMA((4,))]
 
 
 def shape(*dims):
@@ -500,12 +516,8 @@
 
 def to_neighbours(traces):
     xlo, xhi, ylo, yhi = traces
-    return [
-        shift(xhi, "rotor", True),
-        shift(xlo, "rotor", False),
-        shift(yhi, "tower", True),
-        shift(ylo, "tower", False),
-    ]
+    y = [shift(yhi, "tower", True), shift(ylo, "tower", False)]
+    return y + [shift(xhi, "rotor", True), shift(xlo, "rotor", False)]
 
 
 def exchange(x):
@@ -522,10 +534,6 @@
 
 def far(x):
     return pltpu.with_memory_space_constraint(x, pltpu.HBM)
-
-
-def info_specs():
-    return [pl.BlockSpec((1, 1, 16, 256), lambda g: (0, 10, 0, 0))] * 4
 
 
 def table(scale, columns):
@@ -536,28 +544,26 @@
     comps = 10 + (sec == 0)
     return pl.pallas_call(
         partial(trace_kernel, sec),
-        grid=(2,),
-        in_specs=[field_spec(), whole((8, 256)), whole((256, 128)), whole((96, 192))],
-        out_specs=[halo_spec(comps)] * 4,
+        in_specs=[AWAY, HERE, HERE],
+        out_specs=[HERE] * 4,
         out_shape=[shape(2, comps, 16, 256)] * 4,
-        compiler_params=params(16),
+        scratch_shapes=blocks(),
+        compiler_params=pltpu.CompilerParams(vmem_limit_bytes=16 * 2**20),
         cost_estimate=estimate(2),
         name="traces",
-    )(far(field), trow, tcol, jnp.asarray(TRACE))
+    )(far(field), trow, tcol)
 
 
 def first_section(field, req, resp, trow, tcol, halos):
     return pl.pallas_call(
         first_section_kernel,
         grid=(2,),
-        in_specs=[field_spec(), whole((384, 128)), whole((128, 128)), whole((8, 256)), whole((256, 128))]
-        + [whole((64, 256)), whole((96, 192))]
-        + [halo_spec(10)] * 4
-        + info_specs(),
-        out_specs=[field_spec(), field_spec(), whole((128, 128))],
+        in_specs=[AWAY] + [HERE] * 14,
+        out_specs=[AWAY, AWAY, HERE],
         out_shape=[pltpu.HBM(FIELD, F32), pltpu.HBM(FIELD, F32), shape(128, 128)],
         scratch_shapes=[
-            vmem(10, 2, 64, 256),
+            vmem(2, 10, 2, 64, 256),
+            vmem(2, 10, 2, 64, 256),
             vmem(128, 128),
             vmem(640, 512, dtype=BF16),
             vmem(10, 2, 32, 256),
@@ -570,6 +576,10 @@
             vmem(10, 2, 192, 256, dtype=BF16),
             vmem(384, 128),
             vmem(640, 256),
+            vmem(640, 1024, dtype=BF16),
+            *blocks(),
+            pltpu.SemaphoreType.DMA((2, 2, 2)),
+            pltpu.SemaphoreType.DMA((2, 2, 2)),
         ],
         compiler_params=params(28),
         cost_estimate=estimate(10),
@@ -577,14 +587,12 @@
     )(far(field), req, resp, trow, tcol, table(-DT, slice(0, 256)), jnp.asarray(TRACE), *halos, *halos)
 
 
-def inner(field, first, resp, trow, tcol):
-    side_spec = pl.BlockSpec((1, 10, 2, 32, 256), lambda g: (g, 0, 0, 0, 0))
+def inner(field, resp, trow, tcol):
     return pl.pallas_call(
         inner_kernel,
         grid=(2,),
-        in_specs=[field_spec(), field_spec(), whole((128, 128)), whole((8, 256)), whole((256, 128))]
-        + [whole((64, 224)), whole((96, 192))],
-        out_specs=[field_spec(), side_spec, side_spec],
+        in_specs=[AWAY] + [HERE] * 5,
+        out_specs=[HERE] * 3,
         out_shape=[shape(*FIELD), shape(2, 10, 2, 32, 256), shape(2, 10, 2, 32, 256)],
         scratch_shapes=[
             vmem(10, 2, 64, 256),
@@ -593,21 +601,19 @@
             vmem(10, 2, 32, 256),
             vmem(10, 2, 32, 256, dtype=BF16),
             vmem(10, 2, 192, 256, dtype=BF16),
+            *blocks(),
         ],
         compiler_params=params(24),
         cost_estimate=estimate(100),
         name="inner",
-    )(far(field), far(first), resp, trow, tcol, table(-0.5 * DT, slice(0, 224)), jnp.asarray(TRACE))
-
-
-def outer(part, xt, yt, resp, halos, infos):
-    side_spec = pl.BlockSpec((1, 10, 2, 32, 256), lambda g: (g, 0, 0, 0, 0))
+    )(far(field), resp, trow, tcol, table(-0.5 * DT, slice(0, 224)), jnp.asarray(TRACE))
+
+
+def outer(part, first, xt, yt, resp, halos, infos):
     return pl.pallas_call(
         outer_kernel,
         grid=(2,),
-        in_specs=[field_spec(), side_spec, side_spec, whole((128, 128)), whole((64, 32))]
-        + [halo_spec(10)] * 4
-        + info_specs(),
+        in_specs=[HERE] * 14,
         out_specs=field_spec(),
         out_shape=shape(*FIELD),
         scratch_shapes=[
@@ -619,13 +625,13 @@
         compiler_params=params(24),
         cost_estimate=estimate(10),
         name="outer",
-    )(part, xt, yt, resp, table(-0.5 * DT, slice(224, 256)), *halos, *infos)
+    )(part, first, xt, yt, resp, table(-0.5 * DT, slice(224, 256)), *halos, *infos)
 
 
 def on_device(field, owner, donor, target, weight):
     req, trow, tcol = pl.pallas_call(
         request_kernel,
-        out_shape=[shape(384, 128), shape(8, 256), shape(256, 128)],
+        out_shape=[shape(512, 128), shape(8, 256), shape(256, 128)],
         compiler_params=pltpu.CompilerParams(vmem_limit_bytes=16 * 2**20),
         name="request",
     )(
@@ -638,15 +644,11 @@
     infos = to_neighbours(trace_call(0, field, trow, tcol))
     resp = pl.pallas_call(
         interpolate_kernel,
-        grid=(4,),
-        in_specs=[
-            pl.BlockSpec((2, 5, 1, 1, 64, 256), lambda i: (0, 0, i // 2, i % 2, 0, 0)),
-            whole((384, 128)),
-        ],
-        out_specs=whole((128, 128)),
+        in_specs=[AWAY, HERE],
+        out_specs=HERE,
         out_shape=shape(128, 128),
-        scratch_shapes=[vmem(384, 128), vmem(640, 256)],
-        compiler_params=params(16),
+        scratch_shapes=[vmem(384, 128), vmem(640, 256), vmem(640, 1024, dtype=BF16)] + blocks(),
+        compiler_params=pltpu.CompilerParams(vmem_limit_bytes=16 * 2**20),
         cost_estimate=estimate(100),
         name="interpolate",
     )(far(field), req)
@@ -654,8 +656,8 @@
     first, middle, resp = first_section(field, req, resp, trow, tcol, infos)
     resp = exchange(resp)
     halos = to_neighbours(trace_call(1, middle, trow, tcol))
-    part, xt, yt = inner(middle, first, resp, trow, tcol)
-    return outer(part, xt, yt, resp, halos, infos)
+    part, xt, yt = inner(middle, resp, trow, tcol)
+    return outer(part, first, xt, yt, resp, halos, infos)
 
 
 def solution(mesh):

time: 98.2 us -> 91.1 us (0.928)
  the two profiles are of different devices: /device:TPU:14 before, /device:TPU:33 now
where the time goes in v2:
time: 91.1 us; the launch traced here: 90.5 us
  starting transfers between devices  42.9 us (47%)
  Pallas kernels  31.2 us (34%)
  blocking collectives  16.1 us (18%)
    ppermute x8, starting transfers between devices, shift(): return lax.ppermute(x, axis, pairs)  26.7 us
    all_to_all x2, starting transfers between devices, exchange(): return lax.all_to_all(x, AXES, split_axis=0, concat_axis=0, tiled=True)  16.2 us
    all_to_all x1, blocking collectives, exchange(): return lax.all_to_all(x, AXES, split_axis=0, concat_axis=0, tiled=True)  16.1 us
    pallas_call x1, Pallas kernels, first_section(): pl.pallas_call(first_section_kernel, grid=(2,), in_specs=[AWAY] + [HERE]...  10.2 us
    pallas_call x1, Pallas kernels, inner(): pl.pallas_call(inner_kernel, grid=(2,), in_specs=[AWAY] + [HERE] * 5, out...  6.68 us
    pallas_call x2, Pallas kernels, trace_call(): pl.pallas_call(partial(trace_kernel, sec), in_specs=[AWAY, HERE, HERE], o...  5.42 us
    pallas_call x1, Pallas kernels, outer(): pl.pallas_call(outer_kernel, grid=(2,), in_specs=[HERE] * 14, out_specs=f...  4.19 us
    pallas_call x1, Pallas kernels, on_device(): pl.pallas_call(interpolate_kernel, in_specs=[AWAY, HERE], out_specs=HERE,...  2.42 us
  transfers between devices with their start and end apart: 10, of which 0 were waited for; matrix products, arithmetic and copies ran while one was open for 0% of the time, Pallas kernels for 16%

profile of v2, /device:TPU:33, one launch (start us, length us, event | category | flops | bytes accessed | tf_op | source)
XLA Modules:
  0.0 90.5 jit_solution(18088198443301356395)
XLA Ops:
  0.0 2.3 %request.1 = (f32[512,128]{1,0:T(8,128)}, f32[8,256]{1,0:T(8,128)S(1)}, f32[256,128]{1,0:T(8,128)S(1)}) custom-call(s32[2,128]{1,0:T(2,128)} %bitcast.23, s32[2,128]{1,0:T(2,128)} %bitcast.24, s32[2,128]{1,0:T(2,128)} %bitcast.25, f32[2,64,128]{2,1,0:T(8,128)} %bitcast.22), custom_call_target="tpu_custom_call" | custom-call | tf_op jit(solution)/shard_map/request/pallas_call | solution.py:632
  2.3 10.5 %all-to-all-start = ((f32[128,4,128]{2,1,0:T(4,128)}), f32[128,4,128]{2,1,0:T(4,128)S(1)}, u32[]{:S(2)}, u32[]{:S(2)}) async-start(f32[128,4,128]{2,1,0:T(4,128)} %bitcast.5), calls=%async_computation | async-start | bytes 524288 | tf_op jit(solution)/shard_map/all_to_all | solution.py:524
  12.8 2.3 %traces.2 = (f32[2,11,16,256]{3,2,1,0:T(8,128)S(1)}, f32[2,11,16,256]{3,2,1,0:T(8,128)S(1)}, f32[2,11,16,256]{3,2,1,0:T(8,128)S(1)}, f32[2,11,16,256]{3,2,1,0:T(8,128)S(1)}) custom-call(f32[2,5,2,2,64,256]{5,4,3,2,1,0:T(8,128)} %field.5, f32[8,256]{1,0:T(8,128)S(1)} %get-tuple-element.23.trow, f32[256,128]{1,0:T(8,128)S(1)} %get-tuple-element.24.tcol), custom_call_target="tpu_custom_call" | custom-call | flops 2000000000 | bytes 100000 | tf_op jit(solution)/shard_map/traces/pallas_call | solution.py:545
  15.1 3.1 %collective-permute-start = (f32[2,11,16,256]{3,2,1,0:T(8,128)S(1)}, f32[2,11,16,256]{3,2,1,0:T(8,128)S(1)}, u32[]{:S(2)}, u32[]{:S(2)}) collective-permute-start(f32[2,11,16,256]{3,2,1,0:T(8,128)S(1)} %get-tuple-element.25), channel_id=1, source_target_pairs={{0,1},{1,2},{2,3},{3,4},{4,5},{5,6},{6,7},{7,8},{8,9},{9,10},{10,1... | collective-permute-start | bytes 1081352 | tf_op jit(solution)/shard_map/ppermute | solution.py:514
  18.2 4.3 %collective-permute-start.1 = (f32[2,11,16,256]{3,2,1,0:T(8,128)S(1)}, f32[2,11,16,256]{3,2,1,0:T(8,128)S(1)}, u32[]{:S(2)}, u32[]{:S(2)}) collective-permute-start(f32[2,11,16,256]{3,2,1,0:T(8,128)S(1)} %get-tuple-element.26), channel_id=1, source_target_pairs={{1,0},{2,1},{3,2},{4,3},{5,4},{6,5},{7,6},{8,7},{9,8},{10,9},{11,1... | collective-permute-start | bytes 1081352 | tf_op jit(solution)/shard_map/ppermute | solution.py:514
  22.5 4.0 %collective-permute-start.2 = (f32[2,11,16,256]{3,2,1,0:T(8,128)S(1)}, f32[2,11,16,256]{3,2,1,0:T(8,128)S(1)}, u32[]{:S(2)}, u32[]{:S(2)}) collective-permute-start(f32[2,11,16,256]{3,2,1,0:T(8,128)S(1)} %get-tuple-element.27), channel_id=1, source_target_pairs={{0,16},{16,32},{32,48},{48,64},{64,80},{80,96},{96,112},{1,17},{17... | collective-permute-start | bytes 1081352 | tf_op jit(solution)/shard_map/ppermute | solution.py:514
  26.5 1.9 %collective-permute-start.3 = (f32[2,11,16,256]{3,2,1,0:T(8,128)S(1)}, f32[2,11,16,256]{3,2,1,0:T(8,128)S(1)}, u32[]{:S(2)}, u32[]{:S(2)}) collective-permute-start(f32[2,11,16,256]{3,2,1,0:T(8,128)S(1)} %get-tuple-element.28), channel_id=1, source_target_pairs={{16,0},{32,16},{48,32},{64,48},{80,64},{96,80},{112,96},{17,1},{33... | collective-permute-start | bytes 1081352 | tf_op jit(solution)/shard_map/ppermute | solution.py:514
  28.4 0.0 all-to-all-done
  28.4 0.0 copy-start
  28.4 0.0 copy-start.2
  28.4 2.4 %interpolate.1 = f32[128,128]{1,0:T(8,128)S(1)} custom-call(f32[2,5,2,2,64,256]{5,4,3,2,1,0:T(8,128)} %field.5, f32[512,128]{1,0:T(8,128)S(1)} %bitcast.16), custom_call_target="tpu_custom_call" | custom-call | flops 99999997952 | bytes 100000 | tf_op jit(solution)/shard_map/interpolate/pallas_call | solution.py:645
  30.8 16.1 %all_to_all.33 = f32[128,1,128]{2,1,0:T(1,128)S(1)} all-to-all(f32[128,1,128]{2,1,0:T(1,128)S(1)} %bitcast.21), channel_id=1, replica_groups=mesh['rotor'=8,'tower'=16] {'rotor','tower'}, dimensions={0} | all-to-all | bytes 131072 | tf_op jit(solution)/shard_map/all_to_all | solution.py:524
  47.0 0.0 collective-permute-done.refs_0_.refs_4_
  47.0 0.0 collective-permute-done.1.refs_1_.refs_5_
  47.0 0.0 collective-permute-done.2.refs_2_.refs_6_
  47.0 0.0 collective-permute-done.3.refs_3_.refs_7_
  47.0 0.0 copy-done
  47.0 0.0 copy-done.2
  47.0 10.2 %first_section.1 = (f32[2,5,2,2,64,256]{5,4,3,2,1,0:T(8,128)}, f32[2,5,2,2,64,256]{5,4,3,2,1,0:T(8,128)}, f32[128,128]{1,0:T(8,128)}) custom-call(f32[2,5,2,2,64,256]{5,4,3,2,1,0:T(8,128)} %field.5, f32[512,128]{1,0:T(8,128)S(1)} %bitcast.17, f32[128,128]{1,0:T(8,128)S(1)} %bitcast.20, f32[8,256]{1,0:T(8,128)S(1)} %get-tuple-element.23.trow, ...), custom_call_target="tpu_custom_call" | custom-call | flops 10000000000 | bytes 100000 | tf_op jit(solution)/shard_map/first_section/pallas_call | solution.py:558
  57.2 5.6 %all-to-all-start.2 = ((f32[128,1,128]{2,1,0:T(1,128)}), f32[128,1,128]{2,1,0:T(1,128)S(1)}, u32[]{:S(2)}, u32[]{:S(2)}) async-start(f32[128,1,128]{2,1,0:T(1,128)} %bitcast.11), calls=%async_computation.2 | async-start | bytes 131072 | tf_op jit(solution)/shard_map/all_to_all | solution.py:524
  62.9 0.0 copy-start.1
  62.9 3.1 %traces.3 = (f32[2,10,16,256]{3,2,1,0:T(8,128)S(1)}, f32[2,10,16,256]{3,2,1,0:T(8,128)}, f32[2,10,16,256]{3,2,1,0:T(8,128)}, f32[2,10,16,256]{3,2,1,0:T(8,128)}) custom-call(f32[2,5,2,2,64,256]{5,4,3,2,1,0:T(8,128)} %get-tuple-element.29.field, f32[8,256]{1,0:T(8,128)S(1)} %get-tuple-element.23.trow, f32[256,128]{1,0:T(8,128)S(1)} %get-tuple-element.24.tcol), custom_call_target="tpu_custom_call" | custom-call | flops 2000000000 | bytes 100000 | tf_op jit(solution)/shard_map/traces/pallas_call | solution.py:545
  66.1 3.1 %collective-permute-start.4 = (f32[2,10,16,256]{3,2,1,0:T(8,128)}, f32[2,10,16,256]{3,2,1,0:T(8,128)S(1)}, u32[]{:S(2)}, u32[]{:S(2)}) collective-permute-start(f32[2,10,16,256]{3,2,1,0:T(8,128)} %get-tuple-element.35), channel_id=1, source_target_pairs={{0,1},{1,2},{2,3},{3,4},{4,5},{5,6},{6,7},{7,8},{8,9},{9,10},{10,1... | collective-permute-start | bytes 983048 | tf_op jit(solution)/shard_map/ppermute | solution.py:514
  69.2 4.3 %collective-permute-start.5 = (f32[2,10,16,256]{3,2,1,0:T(8,128)}, f32[2,10,16,256]{3,2,1,0:T(8,128)S(1)}, u32[]{:S(2)}, u32[]{:S(2)}) collective-permute-start(f32[2,10,16,256]{3,2,1,0:T(8,128)} %get-tuple-element.36), channel_id=1, source_target_pairs={{1,0},{2,1},{3,2},{4,3},{5,4},{6,5},{7,6},{8,7},{9,8},{10,9},{11,1... | collective-permute-start | bytes 983048 | tf_op jit(solution)/shard_map/ppermute | solution.py:514
  73.5 4.0 %collective-permute-start.6 = (f32[2,10,16,256]{3,2,1,0:T(8,128)}, f32[2,10,16,256]{3,2,1,0:T(8,128)S(1)}, u32[]{:S(2)}, u32[]{:S(2)}) collective-permute-start(f32[2,10,16,256]{3,2,1,0:T(8,128)} %get-tuple-element.37), channel_id=1, source_target_pairs={{0,16},{16,32},{32,48},{48,64},{64,80},{80,96},{96,112},{1,17},{17... | collective-permute-start | bytes 983048 | tf_op jit(solution)/shard_map/ppermute | solution.py:514
  77.4 2.1 %collective-permute-start.7 = (f32[2,10,16,256]{3,2,1,0:T(8,128)S(1)}, f32[2,10,16,256]{3,2,1,0:T(8,128)S(1)}, u32[]{:S(2)}, u32[]{:S(2)}) collective-permute-start(f32[2,10,16,256]{3,2,1,0:T(8,128)S(1)} %get-tuple-element.38), channel_id=1, source_target_pairs={{16,0},{32,16},{48,32},{64,48},{80,64},{96,80},{112,96},{17,1},{33... | collective-permute-start | bytes 983048 | tf_op jit(solution)/shard_map/ppermute | solution.py:514
  79.6 0.0 all-to-all-done.2
  79.6 0.0 copy-done.1
  79.6 0.0 copy-start.3
  79.6 0.0 copy-start.4
  79.6 6.7 %inner.1 = (f32[2,5,2,2,64,256]{5,4,3,2,1,0:T(8,128)S(1)}, f32[2,10,2,32,256]{4,3,2,1,0:T(8,128)S(1)}, f32[2,10,2,32,256]{4,3,2,1,0:T(8,128)S(1)}) custom-call(f32[2,5,2,2,64,256]{5,4,3,2,1,0:T(8,128)} %get-tuple-element.29.field, f32[128,128]{1,0:T(8,128)S(1)} %bitcast.18, f32[8,256]{1,0:T(8,128)S(1)} %get-tuple-element.23.trow, ...), custom_call_target="tpu_custom_call" | custom-call | flops 99999997952 | bytes 100000 | tf_op jit(solution)/shard_map/inner/pallas_call | solution.py:591
  86.3 0.0 collective-permute-done.4.refs_0_
  86.3 0.0 collective-permute-done.5.refs_1_
  86.3 0.0 collective-permute-done.6.refs_2_
  86.3 0.0 collective-permute-done.7.refs_3_
  86.3 0.0 copy-done.3
  86.3 0.0 copy-done.4
  86.3 4.2 %outer.1 = f32[2,5,2,2,64,256]{5,4,3,2,1,0:T(8,128)} custom-call(f32[2,5,2,2,64,256]{5,4,3,2,1,0:T(8,128)S(1)} %get-tuple-element.31.part, f32[2,5,2,2,64,256]{5,4,3,2,1,0:T(8,128)S(1)} %copy-done.4, f32[2,10,2,32,256]{4,3,2,1,0:T(8,128)S(1)} %get-tuple-element.33.xt, f32[2,10,2,32,256]{4,3,2,1,0:T(8,128)S(1)} %get-tuple-element.34.yt, ...), custom_call_target="tpu_custom_call" | custom-call | flops 10000000000 | bytes 100000 | tf_op jit(solution)/shard_map/outer/pallas_call | solution.py:613
Async XLA Ops:
  2.3 26.1 %all-to-all-start = ((f32[128,4,128]{2,1,0:T(4,128)}), f32[128,4,128]{2,1,0:T(4,128)S(1)}, u32[]{:S(2)}, u32[]{:S(2)}) async-start(f32[128,4,128]{2,1,0:T(4,128)} %bitcast.5), calls=%async_computation | async-start | bytes 524288 | tf_op jit(solution)/shard_map/all_to_all | solution.py:524
  15.1 31.9 %collective-permute-start = (f32[2,11,16,256]{3,2,1,0:T(8,128)S(1)}, f32[2,11,16,256]{3,2,1,0:T(8,128)S(1)}, u32[]{:S(2)}, u32[]{:S(2)}) collective-permute-start(f32[2,11,16,256]{3,2,1,0:T(8,128)S(1)} %get-tuple-element.25), channel_id=1, source_target_pairs={{0,1},{1,2},{2,3},{3,4},{4,5},{5,6},{6,7},{7,8},{8,9},{9,10},{10,1... | collective-permute-start | bytes 1081352 | tf_op jit(solution)/shard_map/ppermute | solution.py:514
  18.2 28.8 %collective-permute-start.1 = (f32[2,11,16,256]{3,2,1,0:T(8,128)S(1)}, f32[2,11,16,256]{3,2,1,0:T(8,128)S(1)}, u32[]{:S(2)}, u32[]{:S(2)}) collective-permute-start(f32[2,11,16,256]{3,2,1,0:T(8,128)S(1)} %get-tuple-element.26), channel_id=1, source_target_pairs={{1,0},{2,1},{3,2},{4,3},{5,4},{6,5},{7,6},{8,7},{9,8},{10,9},{11,1... | collective-permute-start | bytes 1081352 | tf_op jit(solution)/shard_map/ppermute | solution.py:514
  22.5 24.5 %collective-permute-start.2 = (f32[2,11,16,256]{3,2,1,0:T(8,128)S(1)}, f32[2,11,16,256]{3,2,1,0:T(8,128)S(1)}, u32[]{:S(2)}, u32[]{:S(2)}) collective-permute-start(f32[2,11,16,256]{3,2,1,0:T(8,128)S(1)} %get-tuple-element.27), channel_id=1, source_target_pairs={{0,16},{16,32},{32,48},{48,64},{64,80},{80,96},{96,112},{1,17},{17... | collective-permute-start | bytes 1081352 | tf_op jit(solution)/shard_map/ppermute | solution.py:514
  26.5 20.5 %collective-permute-start.3 = (f32[2,11,16,256]{3,2,1,0:T(8,128)S(1)}, f32[2,11,16,256]{3,2,1,0:T(8,128)S(1)}, u32[]{:S(2)}, u32[]{:S(2)}) collective-permute-start(f32[2,11,16,256]{3,2,1,0:T(8,128)S(1)} %get-tuple-element.28), channel_id=1, source_target_pairs={{16,0},{32,16},{48,32},{64,48},{80,64},{96,80},{112,96},{17,1},{33... | collective-permute-start | bytes 1081352 | tf_op jit(solution)/shard_map/ppermute | solution.py:514
  28.4 18.6 %copy-start = (bf16[96,192]{1,0:T(8,128)(2,1)S(1)}, bf16[96,192]{1,0:T(8,128)(2,1)}, u32[]{:S(2)}) copy-start(bf16[96,192]{1,0:T(8,128)(2,1)} %constant.9.clone.trace_t) | copy-start | bytes 110596
  28.4 18.6 %copy-start.2 = (bf16[64,256]{1,0:T(8,128)(2,1)S(1)}, bf16[64,256]{1,0:T(8,128)(2,1)}, u32[]{:S(2)}) copy-start(bf16[64,256]{1,0:T(8,128)(2,1)} %constant.8.clone.main_t) | copy-start | bytes 98308
  57.2 22.3 %all-to-all-start.2 = ((f32[128,1,128]{2,1,0:T(1,128)}), f32[128,1,128]{2,1,0:T(1,128)S(1)}, u32[]{:S(2)}, u32[]{:S(2)}) async-start(f32[128,1,128]{2,1,0:T(1,128)} %bitcast.11), calls=%async_computation.2 | async-start | bytes 131072 | tf_op jit(solution)/shard_map/all_to_all | solution.py:524
  62.9 16.7 %copy-start.1 = (bf16[64,224]{1,0:T(8,128)(2,1)S(1)}, bf16[64,224]{1,0:T(8,128)(2,1)}, u32[]{:S(2)}) copy-start(bf16[64,224]{1,0:T(8,128)(2,1)} %constant.10.clone.main_t) | copy-start | bytes 86020
  66.1 20.2 %collective-permute-start.4 = (f32[2,10,16,256]{3,2,1,0:T(8,128)}, f32[2,10,16,256]{3,2,1,0:T(8,128)S(1)}, u32[]{:S(2)}, u32[]{:S(2)}) collective-permute-start(f32[2,10,16,256]{3,2,1,0:T(8,128)} %get-tuple-element.35), channel_id=1, source_target_pairs={{0,1},{1,2},{2,3},{3,4},{4,5},{5,6},{6,7},{7,8},{8,9},{9,10},{10,1... | collective-permute-start | bytes 983048 | tf_op jit(solution)/shard_map/ppermute | solution.py:514
  69.2 17.1 %collective-permute-start.5 = (f32[2,10,16,256]{3,2,1,0:T(8,128)}, f32[2,10,16,256]{3,2,1,0:T(8,128)S(1)}, u32[]{:S(2)}, u32[]{:S(2)}) collective-permute-start(f32[2,10,16,256]{3,2,1,0:T(8,128)} %get-tuple-element.36), channel_id=1, source_target_pairs={{1,0},{2,1},{3,2},{4,3},{5,4},{6,5},{7,6},{8,7},{9,8},{10,9},{11,1... | collective-permute-start | bytes 983048 | tf_op jit(solution)/shard_map/ppermute | solution.py:514
  73.5 12.8 %collective-permute-start.6 = (f32[2,10,16,256]{3,2,1,0:T(8,128)}, f32[2,10,16,256]{3,2,1,0:T(8,128)S(1)}, u32[]{:S(2)}, u32[]{:S(2)}) collective-permute-start(f32[2,10,16,256]{3,2,1,0:T(8,128)} %get-tuple-element.37), channel_id=1, source_target_pairs={{0,16},{16,32},{32,48},{48,64},{64,80},{80,96},{96,112},{1,17},{17... | collective-permute-start | bytes 983048 | tf_op jit(solution)/shard_map/ppermute | solution.py:514
  77.4 8.9 %collective-permute-start.7 = (f32[2,10,16,256]{3,2,1,0:T(8,128)S(1)}, f32[2,10,16,256]{3,2,1,0:T(8,128)S(1)}, u32[]{:S(2)}, u32[]{:S(2)}) collective-permute-start(f32[2,10,16,256]{3,2,1,0:T(8,128)S(1)} %get-tuple-element.38), channel_id=1, source_target_pairs={{16,0},{32,16},{48,32},{64,48},{80,64},{96,80},{112,96},{17,1},{33... | collective-permute-start | bytes 983048 | tf_op jit(solution)/shard_map/ppermute | solution.py:514
  79.6 6.8 %copy-start.3 = (bf16[64,32]{1,0:T(8,128)(2,1)S(1)}, bf16[64,32]{1,0:T(8,128)(2,1)}, u32[]{:S(2)}) copy-start(bf16[64,32]{1,0:T(8,128)(2,1)} %constant.11.clone.lift_y) | copy-start | bytes 12292
  79.6 6.8 %copy-start.4 = (f32[2,5,2,2,64,256]{5,4,3,2,1,0:T(8,128)S(1)}, f32[2,5,2,2,64,256]{5,4,3,2,1,0:T(8,128)}, u32[]{:S(2)}) copy-start(f32[2,5,2,2,64,256]{5,4,3,2,1,0:T(8,128)} %get-tuple-element.32.first) | copy-start | bytes 7864324

commit v3 on v2

--- a/solution.py
+++ b/solution.py
@@ -272,14 +272,12 @@
     val = values(got, 0)
     at = iota((64, 256), 0) + 64 * g == point_row(trow, sec)
     for c in range(10):
-        hi, lo = split(jnp.where(at, val[c : c + 1], 0.0))
-        lhs[64 * c : 64 * c + 64, 0:256] = hi
-        lhs[64 * c : 64 * c + 64, 256:512] = lo
+        lhs[64 * c : 64 * c + 64, :] = jnp.where(at, val[c : c + 1], 0.0).astype(BF16)
     where = jnp.where(iota((256, 512), 1) == element_col(tcol, sec, 512), 1.0, 0.0).astype(BF16)
     mask = dot(jnp.where(at, 1.0, 0.0).astype(BF16), where)
     for x in range(2):
         wx = where[:, x * 256 : x * 256 + 256]
-        scat = dot(lhs[...], jnp.concatenate([wx, wx], axis=0))
+        scat = dot(lhs[...], wx)
         block_in(field, buf, sem, 2 * g + x).wait()
         hit = mask[:, x * 256 : x * 256 + 256] > 0.5
         for c in range(10):
@@ -546,7 +544,7 @@
         partial(trace_kernel, sec),
         in_specs=[AWAY, HERE, HERE],
         out_specs=[HERE] * 4,
-        out_shape=[shape(2, comps, 16, 256)] * 4,
+        out_shape=[pltpu.VMEM((2, comps, 16, 256), F32)] * 4,
         scratch_shapes=blocks(),
         compiler_params=pltpu.CompilerParams(vmem_limit_bytes=16 * 2**20),
         cost_estimate=estimate(2),
@@ -565,7 +563,7 @@
             vmem(2, 10, 2, 64, 256),
             vmem(2, 10, 2, 64, 256),
             vmem(128, 128),
-            vmem(640, 512, dtype=BF16),
+            vmem(640, 256, dtype=BF16),
             vmem(10, 2, 32, 256),
             vmem(10, 2, 32, 256),
             vmem(10, 2, 32, 256),
@@ -597,7 +595,7 @@
         scratch_shapes=[
             vmem(10, 2, 64, 256),
             vmem(128, 128),
-            vmem(640, 512, dtype=BF16),
+            vmem(640, 256, dtype=BF16),
             vmem(10, 2, 32, 256),
             vmem(10, 2, 32, 256, dtype=BF16),
             vmem(10, 2, 192, 256, dtype=BF16),

time: 91.1 us -> 90.1 us (0.989)
  Pallas kernels: 31.2 us -> 30.2 us
where the time goes in v3:
time: 90.1 us; the launch traced here: 89.5 us
  starting transfers between devices  42.9 us (48%)
  Pallas kernels  30.2 us (34%)
  blocking collectives  16.1 us (18%)
    ppermute x8, starting transfers between devices, shift(): return lax.ppermute(x, axis, pairs)  26.7 us
    all_to_all x2, starting transfers between devices, exchange(): return lax.all_to_all(x, AXES, split_axis=0, concat_axis=0, tiled=True)  16.2 us
    all_to_all x1, blocking collectives, exchange(): return lax.all_to_all(x, AXES, split_axis=0, concat_axis=0, tiled=True)  16.1 us
    pallas_call x1, Pallas kernels, first_section(): pl.pallas_call(first_section_kernel, grid=(2,), in_specs=[AWAY] + [HERE]...  9.71 us
    pallas_call x1, Pallas kernels, inner(): pl.pallas_call(inner_kernel, grid=(2,), in_specs=[AWAY] + [HERE] * 5, out...  6.19 us
    pallas_call x2, Pallas kernels, trace_call(): pl.pallas_call(partial(trace_kernel, sec), in_specs=[AWAY, HERE, HERE], o...  5.42 us
    pallas_call x1, Pallas kernels, outer(): pl.pallas_call(outer_kernel, grid=(2,), in_specs=[HERE] * 14, out_specs=f...  4.18 us
    pallas_call x1, Pallas kernels, on_device(): pl.pallas_call(interpolate_kernel, in_specs=[AWAY, HERE], out_specs=HERE,...  2.42 us
  transfers between devices with their start and end apart: 10, of which 0 were waited for; matrix products, arithmetic and copies ran while one was open for 0% of the time, Pallas kernels for 16%

profile of v3, /device:TPU:33, one launch (start us, length us, event | category | flops | bytes accessed | tf_op | source)
XLA Modules:
  0.0 89.5 jit_solution(14961855646669229729)
XLA Ops:
  0.0 2.3 %request.1 = (f32[512,128]{1,0:T(8,128)}, f32[8,256]{1,0:T(8,128)S(1)}, f32[256,128]{1,0:T(8,128)S(1)}) custom-call(s32[2,128]{1,0:T(2,128)} %bitcast.23, s32[2,128]{1,0:T(2,128)} %bitcast.24, s32[2,128]{1,0:T(2,128)} %bitcast.25, f32[2,64,128]{2,1,0:T(8,128)} %bitcast.22), custom_call_target="tpu_custom_call" | custom-call | tf_op jit(solution)/shard_map/request/pallas_call | solution.py:630
  2.3 10.5 %all-to-all-start = ((f32[128,4,128]{2,1,0:T(4,128)}), f32[128,4,128]{2,1,0:T(4,128)S(1)}, u32[]{:S(2)}, u32[]{:S(2)}) async-start(f32[128,4,128]{2,1,0:T(4,128)} %bitcast.5), calls=%async_computation | async-start | bytes 524288 | tf_op jit(solution)/shard_map/all_to_all | solution.py:522
  12.8 2.3 %traces.2 = (f32[2,11,16,256]{3,2,1,0:T(8,128)S(1)}, f32[2,11,16,256]{3,2,1,0:T(8,128)S(1)}, f32[2,11,16,256]{3,2,1,0:T(8,128)S(1)}, f32[2,11,16,256]{3,2,1,0:T(8,128)S(1)}) custom-call(f32[2,5,2,2,64,256]{5,4,3,2,1,0:T(8,128)} %field.5, f32[8,256]{1,0:T(8,128)S(1)} %get-tuple-element.23.trow, f32[256,128]{1,0:T(8,128)S(1)} %get-tuple-element.24.tcol), custom_call_target="tpu_custom_call" | custom-call | flops 2000000000 | bytes 100000 | tf_op jit(solution)/shard_map/traces/pallas_call | solution.py:543
  15.1 3.1 %collective-permute-start = (f32[2,11,16,256]{3,2,1,0:T(8,128)S(1)}, f32[2,11,16,256]{3,2,1,0:T(8,128)S(1)}, u32[]{:S(2)}, u32[]{:S(2)}) collective-permute-start(f32[2,11,16,256]{3,2,1,0:T(8,128)S(1)} %get-tuple-element.25), channel_id=1, source_target_pairs={{0,1},{1,2},{2,3},{3,4},{4,5},{5,6},{6,7},{7,8},{8,9},{9,10},{10,1... | collective-permute-start | bytes 1081352 | tf_op jit(solution)/shard_map/ppermute | solution.py:512
  18.2 4.3 %collective-permute-start.1 = (f32[2,11,16,256]{3,2,1,0:T(8,128)S(1)}, f32[2,11,16,256]{3,2,1,0:T(8,128)S(1)}, u32[]{:S(2)}, u32[]{:S(2)}) collective-permute-start(f32[2,11,16,256]{3,2,1,0:T(8,128)S(1)} %get-tuple-element.26), channel_id=1, source_target_pairs={{1,0},{2,1},{3,2},{4,3},{5,4},{6,5},{7,6},{8,7},{9,8},{10,9},{11,1... | collective-permute-start | bytes 1081352 | tf_op jit(solution)/shard_map/ppermute | solution.py:512
  22.5 4.0 %collective-permute-start.2 = (f32[2,11,16,256]{3,2,1,0:T(8,128)S(1)}, f32[2,11,16,256]{3,2,1,0:T(8,128)S(1)}, u32[]{:S(2)}, u32[]{:S(2)}) collective-permute-start(f32[2,11,16,256]{3,2,1,0:T(8,128)S(1)} %get-tuple-element.27), channel_id=1, source_target_pairs={{0,16},{16,32},{32,48},{48,64},{64,80},{80,96},{96,112},{1,17},{17... | collective-permute-start | bytes 1081352 | tf_op jit(solution)/shard_map/ppermute | solution.py:512
  26.5 1.9 %collective-permute-start.3 = (f32[2,11,16,256]{3,2,1,0:T(8,128)S(1)}, f32[2,11,16,256]{3,2,1,0:T(8,128)S(1)}, u32[]{:S(2)}, u32[]{:S(2)}) collective-permute-start(f32[2,11,16,256]{3,2,1,0:T(8,128)S(1)} %get-tuple-element.28), channel_id=1, source_target_pairs={{16,0},{32,16},{48,32},{64,48},{80,64},{96,80},{112,96},{17,1},{33... | collective-permute-start | bytes 1081352 | tf_op jit(solution)/shard_map/ppermute | solution.py:512
  28.4 0.0 all-to-all-done
  28.4 0.0 copy-start
  28.4 0.0 copy-start.2
  28.4 2.4 %interpolate.1 = f32[128,128]{1,0:T(8,128)S(1)} custom-call(f32[2,5,2,2,64,256]{5,4,3,2,1,0:T(8,128)} %field.5, f32[512,128]{1,0:T(8,128)S(1)} %bitcast.16), custom_call_target="tpu_custom_call" | custom-call | flops 99999997952 | bytes 100000 | tf_op jit(solution)/shard_map/interpolate/pallas_call | solution.py:643
  30.8 16.1 %all_to_all.33 = f32[128,1,128]{2,1,0:T(1,128)S(1)} all-to-all(f32[128,1,128]{2,1,0:T(1,128)S(1)} %bitcast.21), channel_id=1, replica_groups=mesh['rotor'=8,'tower'=16] {'rotor','tower'}, dimensions={0} | all-to-all | bytes 131072 | tf_op jit(solution)/shard_map/all_to_all | solution.py:522
  47.0 0.0 collective-permute-done.refs_0_.refs_4_
  47.0 0.0 collective-permute-done.1.refs_1_.refs_5_
  47.0 0.0 collective-permute-done.2.refs_2_.refs_6_
  47.0 0.0 collective-permute-done.3.refs_3_.refs_7_
  47.0 0.0 copy-done
  47.0 0.0 copy-done.2
  47.0 9.7 %first_section.1 = (f32[2,5,2,2,64,256]{5,4,3,2,1,0:T(8,128)}, f32[2,5,2,2,64,256]{5,4,3,2,1,0:T(8,128)}, f32[128,128]{1,0:T(8,128)}) custom-call(f32[2,5,2,2,64,256]{5,4,3,2,1,0:T(8,128)} %field.5, f32[512,128]{1,0:T(8,128)S(1)} %bitcast.17, f32[128,128]{1,0:T(8,128)S(1)} %bitcast.20, f32[8,256]{1,0:T(8,128)S(1)} %get-tuple-element.23.trow, ...), custom_call_target="tpu_custom_call" | custom-call | flops 10000000000 | bytes 100000 | tf_op jit(solution)/shard_map/first_section/pallas_call | solution.py:556
  56.7 5.6 %all-to-all-start.2 = ((f32[128,1,128]{2,1,0:T(1,128)}), f32[128,1,128]{2,1,0:T(1,128)S(1)}, u32[]{:S(2)}, u32[]{:S(2)}) async-start(f32[128,1,128]{2,1,0:T(1,128)} %bitcast.11), calls=%async_computation.2 | async-start | bytes 131072 | tf_op jit(solution)/shard_map/all_to_all | solution.py:522
  62.4 0.0 copy-start.1
  62.4 3.1 %traces.3 = (f32[2,10,16,256]{3,2,1,0:T(8,128)S(1)}, f32[2,10,16,256]{3,2,1,0:T(8,128)}, f32[2,10,16,256]{3,2,1,0:T(8,128)}, f32[2,10,16,256]{3,2,1,0:T(8,128)}) custom-call(f32[2,5,2,2,64,256]{5,4,3,2,1,0:T(8,128)} %get-tuple-element.29.field, f32[8,256]{1,0:T(8,128)S(1)} %get-tuple-element.23.trow, f32[256,128]{1,0:T(8,128)S(1)} %get-tuple-element.24.tcol), custom_call_target="tpu_custom_call" | custom-call | flops 2000000000 | bytes 100000 | tf_op jit(solution)/shard_map/traces/pallas_call | solution.py:543
  65.6 3.1 %collective-permute-start.4 = (f32[2,10,16,256]{3,2,1,0:T(8,128)}, f32[2,10,16,256]{3,2,1,0:T(8,128)S(1)}, u32[]{:S(2)}, u32[]{:S(2)}) collective-permute-start(f32[2,10,16,256]{3,2,1,0:T(8,128)} %get-tuple-element.35), channel_id=1, source_target_pairs={{0,1},{1,2},{2,3},{3,4},{4,5},{5,6},{6,7},{7,8},{8,9},{9,10},{10,1... | collective-permute-start | bytes 983048 | tf_op jit(solution)/shard_map/ppermute | solution.py:512
  68.7 4.3 %collective-permute-start.5 = (f32[2,10,16,256]{3,2,1,0:T(8,128)}, f32[2,10,16,256]{3,2,1,0:T(8,128)S(1)}, u32[]{:S(2)}, u32[]{:S(2)}) collective-permute-start(f32[2,10,16,256]{3,2,1,0:T(8,128)} %get-tuple-element.36), channel_id=1, source_target_pairs={{1,0},{2,1},{3,2},{4,3},{5,4},{6,5},{7,6},{8,7},{9,8},{10,9},{11,1... | collective-permute-start | bytes 983048 | tf_op jit(solution)/shard_map/ppermute | solution.py:512
  73.0 4.0 %collective-permute-start.6 = (f32[2,10,16,256]{3,2,1,0:T(8,128)}, f32[2,10,16,256]{3,2,1,0:T(8,128)S(1)}, u32[]{:S(2)}, u32[]{:S(2)}) collective-permute-start(f32[2,10,16,256]{3,2,1,0:T(8,128)} %get-tuple-element.37), channel_id=1, source_target_pairs={{0,16},{16,32},{32,48},{48,64},{64,80},{80,96},{96,112},{1,17},{17... | collective-permute-start | bytes 983048 | tf_op jit(solution)/shard_map/ppermute | solution.py:512
  76.9 2.1 %collective-permute-start.7 = (f32[2,10,16,256]{3,2,1,0:T(8,128)S(1)}, f32[2,10,16,256]{3,2,1,0:T(8,128)S(1)}, u32[]{:S(2)}, u32[]{:S(2)}) collective-permute-start(f32[2,10,16,256]{3,2,1,0:T(8,128)S(1)} %get-tuple-element.38), channel_id=1, source_target_pairs={{16,0},{32,16},{48,32},{64,48},{80,64},{96,80},{112,96},{17,1},{33... | collective-permute-start | bytes 983048 | tf_op jit(solution)/shard_map/ppermute | solution.py:512
  79.0 0.0 all-to-all-done.2
  79.0 0.0 copy-done.1
  79.1 0.0 copy-start.3
  79.1 0.0 copy-start.4
  79.1 6.2 %inner.1 = (f32[2,5,2,2,64,256]{5,4,3,2,1,0:T(8,128)S(1)}, f32[2,10,2,32,256]{4,3,2,1,0:T(8,128)S(1)}, f32[2,10,2,32,256]{4,3,2,1,0:T(8,128)S(1)}) custom-call(f32[2,5,2,2,64,256]{5,4,3,2,1,0:T(8,128)} %get-tuple-element.29.field, f32[128,128]{1,0:T(8,128)S(1)} %bitcast.18, f32[8,256]{1,0:T(8,128)S(1)} %get-tuple-element.23.trow, ...), custom_call_target="tpu_custom_call" | custom-call | flops 99999997952 | bytes 100000 | tf_op jit(solution)/shard_map/inner/pallas_call | solution.py:589
  85.3 0.0 collective-permute-done.4.refs_0_
  85.3 0.0 collective-permute-done.5.refs_1_
  85.3 0.0 collective-permute-done.6.refs_2_
  85.3 0.0 collective-permute-done.7.refs_3_
  85.3 0.0 copy-done.3
  85.3 0.0 copy-done.4
  85.3 4.2 %outer.1 = f32[2,5,2,2,64,256]{5,4,3,2,1,0:T(8,128)} custom-call(f32[2,5,2,2,64,256]{5,4,3,2,1,0:T(8,128)S(1)} %get-tuple-element.31.part, f32[2,5,2,2,64,256]{5,4,3,2,1,0:T(8,128)S(1)} %copy-done.4, f32[2,10,2,32,256]{4,3,2,1,0:T(8,128)S(1)} %get-tuple-element.33.xt, f32[2,10,2,32,256]{4,3,2,1,0:T(8,128)S(1)} %get-tuple-element.34.yt, ...), custom_call_target="tpu_custom_call" | custom-call | flops 10000000000 | bytes 100000 | tf_op jit(solution)/shard_map/outer/pallas_call | solution.py:611
Async XLA Ops:
  2.3 26.1 %all-to-all-start = ((f32[128,4,128]{2,1,0:T(4,128)}), f32[128,4,128]{2,1,0:T(4,128)S(1)}, u32[]{:S(2)}, u32[]{:S(2)}) async-start(f32[128,4,128]{2,1,0:T(4,128)} %bitcast.5), calls=%async_computation | async-start | bytes 524288 | tf_op jit(solution)/shard_map/all_to_all | solution.py:522
  15.1 31.9 %collective-permute-start = (f32[2,11,16,256]{3,2,1,0:T(8,128)S(1)}, f32[2,11,16,256]{3,2,1,0:T(8,128)S(1)}, u32[]{:S(2)}, u32[]{:S(2)}) collective-permute-start(f32[2,11,16,256]{3,2,1,0:T(8,128)S(1)} %get-tuple-element.25), channel_id=1, source_target_pairs={{0,1},{1,2},{2,3},{3,4},{4,5},{5,6},{6,7},{7,8},{8,9},{9,10},{10,1... | collective-permute-start | bytes 1081352 | tf_op jit(solution)/shard_map/ppermute | solution.py:512
  18.2 28.8 %collective-permute-start.1 = (f32[2,11,16,256]{3,2,1,0:T(8,128)S(1)}, f32[2,11,16,256]{3,2,1,0:T(8,128)S(1)}, u32[]{:S(2)}, u32[]{:S(2)}) collective-permute-start(f32[2,11,16,256]{3,2,1,0:T(8,128)S(1)} %get-tuple-element.26), channel_id=1, source_target_pairs={{1,0},{2,1},{3,2},{4,3},{5,4},{6,5},{7,6},{8,7},{9,8},{10,9},{11,1... | collective-permute-start | bytes 1081352 | tf_op jit(solution)/shard_map/ppermute | solution.py:512
  22.5 24.5 %collective-permute-start.2 = (f32[2,11,16,256]{3,2,1,0:T(8,128)S(1)}, f32[2,11,16,256]{3,2,1,0:T(8,128)S(1)}, u32[]{:S(2)}, u32[]{:S(2)}) collective-permute-start(f32[2,11,16,256]{3,2,1,0:T(8,128)S(1)} %get-tuple-element.27), channel_id=1, source_target_pairs={{0,16},{16,32},{32,48},{48,64},{64,80},{80,96},{96,112},{1,17},{17... | collective-permute-start | bytes 1081352 | tf_op jit(solution)/shard_map/ppermute | solution.py:512
  26.5 20.5 %collective-permute-start.3 = (f32[2,11,16,256]{3,2,1,0:T(8,128)S(1)}, f32[2,11,16,256]{3,2,1,0:T(8,128)S(1)}, u32[]{:S(2)}, u32[]{:S(2)}) collective-permute-start(f32[2,11,16,256]{3,2,1,0:T(8,128)S(1)} %get-tuple-element.28), channel_id=1, source_target_pairs={{16,0},{32,16},{48,32},{64,48},{80,64},{96,80},{112,96},{17,1},{33... | collective-permute-start | bytes 1081352 | tf_op jit(solution)/shard_map/ppermute | solution.py:512
  28.4 18.6 %copy-start = (bf16[96,192]{1,0:T(8,128)(2,1)S(1)}, bf16[96,192]{1,0:T(8,128)(2,1)}, u32[]{:S(2)}) copy-start(bf16[96,192]{1,0:T(8,128)(2,1)} %constant.9.clone.trace_t) | copy-start | bytes 110596
  28.4 18.6 %copy-start.2 = (bf16[64,256]{1,0:T(8,128)(2,1)S(1)}, bf16[64,256]{1,0:T(8,128)(2,1)}, u32[]{:S(2)}) copy-start(bf16[64,256]{1,0:T(8,128)(2,1)} %constant.8.clone.main_t) | copy-start | bytes 98308
  56.7 22.3 %all-to-all-start.2 = ((f32[128,1,128]{2,1,0:T(1,128)}), f32[128,1,128]{2,1,0:T(1,128)S(1)}, u32[]{:S(2)}, u32[]{:S(2)}) async-start(f32[128,1,128]{2,1,0:T(1,128)} %bitcast.11), calls=%async_computation.2 | async-start | bytes 131072 | tf_op jit(solution)/shard_map/all_to_all | solution.py:522
  62.4 16.7 %copy-start.1 = (bf16[64,224]{1,0:T(8,128)(2,1)S(1)}, bf16[64,224]{1,0:T(8,128)(2,1)}, u32[]{:S(2)}) copy-start(bf16[64,224]{1,0:T(8,128)(2,1)} %constant.10.clone.main_t) | copy-start | bytes 86020
  65.6 19.7 %collective-permute-start.4 = (f32[2,10,16,256]{3,2,1,0:T(8,128)}, f32[2,10,16,256]{3,2,1,0:T(8,128)S(1)}, u32[]{:S(2)}, u32[]{:S(2)}) collective-permute-start(f32[2,10,16,256]{3,2,1,0:T(8,128)} %get-tuple-element.35), channel_id=1, source_target_pairs={{0,1},{1,2},{2,3},{3,4},{4,5},{5,6},{6,7},{7,8},{8,9},{9,10},{10,1... | collective-permute-start | bytes 983048 | tf_op jit(solution)/shard_map/ppermute | solution.py:512
  68.7 16.6 %collective-permute-start.5 = (f32[2,10,16,256]{3,2,1,0:T(8,128)}, f32[2,10,16,256]{3,2,1,0:T(8,128)S(1)}, u32[]{:S(2)}, u32[]{:S(2)}) collective-permute-start(f32[2,10,16,256]{3,2,1,0:T(8,128)} %get-tuple-element.36), channel_id=1, source_target_pairs={{1,0},{2,1},{3,2},{4,3},{5,4},{6,5},{7,6},{8,7},{9,8},{10,9},{11,1... | collective-permute-start | bytes 983048 | tf_op jit(solution)/shard_map/ppermute | solution.py:512
  73.0 12.3 %collective-permute-start.6 = (f32[2,10,16,256]{3,2,1,0:T(8,128)}, f32[2,10,16,256]{3,2,1,0:T(8,128)S(1)}, u32[]{:S(2)}, u32[]{:S(2)}) collective-permute-start(f32[2,10,16,256]{3,2,1,0:T(8,128)} %get-tuple-element.37), channel_id=1, source_target_pairs={{0,16},{16,32},{32,48},{48,64},{64,80},{80,96},{96,112},{1,17},{17... | collective-permute-start | bytes 983048 | tf_op jit(solution)/shard_map/ppermute | solution.py:512
  76.9 8.4 %collective-permute-start.7 = (f32[2,10,16,256]{3,2,1,0:T(8,128)S(1)}, f32[2,10,16,256]{3,2,1,0:T(8,128)S(1)}, u32[]{:S(2)}, u32[]{:S(2)}) collective-permute-start(f32[2,10,16,256]{3,2,1,0:T(8,128)S(1)} %get-tuple-element.38), channel_id=1, source_target_pairs={{16,0},{32,16},{48,32},{64,48},{80,64},{96,80},{112,96},{17,1},{33... | collective-permute-start | bytes 983048 | tf_op jit(solution)/shard_map/ppermute | solution.py:512
  79.1 6.3 %copy-start.3 = (bf16[64,32]{1,0:T(8,128)(2,1)S(1)}, bf16[64,32]{1,0:T(8,128)(2,1)}, u32[]{:S(2)}) copy-start(bf16[64,32]{1,0:T(8,128)(2,1)} %constant.11.clone.lift_y) | copy-start | bytes 12292
  79.1 6.3 %copy-start.4 = (f32[2,5,2,2,64,256]{5,4,3,2,1,0:T(8,128)S(1)}, f32[2,5,2,2,64,256]{5,4,3,2,1,0:T(8,128)}, u32[]{:S(2)}) copy-start(f32[2,5,2,2,64,256]{5,4,3,2,1,0:T(8,128)} %get-tuple-element.32.first) | copy-start | bytes 7864324
